TPU v7x, 32 devices: a whole 2x2x4 slice. The times are simulated.
32 devices in a mesh: shard: 4 (over z), ctx: 2 (over x), tp: 4 (over y, core).
Axes of the slice: x: 2, y: 2, z: 4, core: 2. Of those that a mesh axis runs over, the one named last changes fastest.
Arguments:
- inputs: float32 [4, 4096, 1536], P('shard', 'ctx'), may hold values from -6 to 6
- lengths: int32 [4], P('shard'), may hold values from 1024 to 4096, as said below
- rec_proj: float32 [1536, 2048], P(('shard', 'ctx'), 'tp'), may hold values from -0.15625 to 0.15625
- gate_proj: float32 [1536, 2048], P(('shard', 'ctx'), 'tp'), may hold values from -0.15625 to 0.15625
- out_proj: float32 [1536, 2048], P(('shard', 'ctx'), 'tp'), may hold values from -0.125 to 0.125
- ffn_gate: float32 [1536, 4608], P(('shard', 'ctx'), 'tp'), may hold values from -0.15625 to 0.15625
- ffn_up: float32 [1536, 4608], P(('shard', 'ctx'), 'tp'), may hold values from -0.15625 to 0.15625
- ffn_down: float32 [1536, 4608], P(('shard', 'ctx'), 'tp'), may hold values from -0.09375 to 0.09375
- conv_weight: float32 [4, 2048], P(None, 'tp'), may hold values from -3 to 3
- conv_bias: float32 [2048], P('tp'), may hold values from -3 to 3
- a_gate: float32 [16, 128, 128], P('tp'), may hold values from -0.5 to 0.5
- i_gate: float32 [16, 128, 128], P('tp'), may hold values from -0.5 to 0.5
- a_bias: float32 [2048], P('tp'), may hold values from -4 to 4
- i_bias: float32 [2048], P('tp'), may hold values from -4 to 4
- lambda_param: float32 [2048], P('tp'), may hold values from 3 to 8
- rec_norm: float32 [1536], replicated, may hold values from 0.1 to 1.9
- ffn_norm: float32 [1536], replicated, may hold values from 0.1 to 1.9
- cotangent: float32 [4, 4096, 1536], P('shard', 'ctx'), may hold values from -6 to 6
Outputs:
- block_out: float32 [4, 4096, 1536], P('shard', 'ctx')
- input_grad: float32 [4, 4096, 1536], P('shard', 'ctx')
- grad_rec_proj: float32 [1536, 2048], P(('shard', 'ctx'), 'tp')
- grad_gate_proj: float32 [1536, 2048], P(('shard', 'ctx'), 'tp')
- grad_out_proj: float32 [1536, 2048], P(('shard', 'ctx'), 'tp')
- grad_ffn_gate: float32 [1536, 4608], P(('shard', 'ctx'), 'tp')
- grad_ffn_up: float32 [1536, 4608], P(('shard', 'ctx'), 'tp')
- grad_ffn_down: float32 [1536, 4608], P(('shard', 'ctx'), 'tp')
- grad_conv_weight: float32 [4, 2048], P(None, 'tp')
- grad_conv_bias: float32 [2048], P('tp')
- grad_a_gate: float32 [16, 128, 128], P('tp')
- grad_i_gate: float32 [16, 128, 128], P('tp')
- grad_a_bias: float32 [2048], P('tp')
- grad_i_bias: float32 [2048], P('tp')
- grad_lambda: float32 [2048], P('tp')
- grad_rec_norm: float32 [1536], replicated
- grad_ffn_norm: float32 [1536], replicated
Inputs may be any that keep to these rules, and one draw needn't show every extreme that they name: `lengths`: in each aligned group of 1 sequence, one drawn from the seed has length 4096.
All inputs are finite; a program needn't handle non-finite values.
Results may differ from a plain program's by a relative error of at most 0.0003.
Values sent between devices are 32-bit elements; how exact they have to be, the bound alone decides.
No kernel may reach another device: no remote copies, remote signals or barrier semaphores. Data moves between devices by JAX's collectives and lax.ppermute only.
A program may use at most 320 MiB of HBM per device.

v0:
```python
import jax
import jax.numpy as jnp
from jax import lax
from jax.sharding import PartitionSpec as P

HIGHEST = lax.Precision.HIGHEST
EPSILON = 1e-06
DECAY_CONST = 8.0


def passed_along(block, axis, distance):
    devices = range(lax.axis_size(axis))
    route = [(i - distance, i) for i in devices if i - distance in devices]
    return lax.ppermute(block, axis, route)


def carried_in(value, axis, join, neutral, backward):
    count, mine = (lax.axis_size(axis), lax.axis_index(axis))
    pieces = jax.tree.map(lambda part: lax.all_gather(part, axis), value)
    if backward:
        pieces = jax.tree.map(lambda part: part[::-1], pieces)
        mine = count - 1 - mine
    so_far = jax.tree.map(
        lambda part, zero: jnp.full_like(part, 0) + jnp.asarray(zero, part.dtype), value, neutral
    )

    def step(position, so_far):
        longer = join(so_far, jax.tree.map(lambda part: part[position], pieces))
        return jax.tree.map(lambda new, old: jnp.where(position < mine, new, old), longer, so_far)

    return lax.fori_loop(0, count - 1, step, so_far)


def affine_pair(earlier, later_pair):
    return (earlier[0] * later_pair[0], later_pair[0] * earlier[1] + later_pair[1])


def matmul(left, right):
    return jnp.dot(left, right, precision=HIGHEST, preferred_element_type=jnp.float32)


def matmul_nt(left, right):
    return lax.dot_general(
        left, right, (((1,), (1,)), ((), ())), precision=HIGHEST, preferred_element_type=jnp.float32
    )


def matmul_tn(left, right):
    return lax.dot_general(
        left, right, (((0,), (0,)), ((), ())), precision=HIGHEST, preferred_element_type=jnp.float32
    )


def gelu_tanh(values):
    return jax.nn.gelu(values, approximate=True)


def gather_recurrent(rec_proj, gate_proj, out_proj):
    return (
        lax.all_gather(rec_proj, ("shard", "ctx"), axis=0, tiled=True),
        lax.all_gather(gate_proj, ("shard", "ctx"), axis=0, tiled=True),
        lax.all_gather(out_proj, ("shard", "ctx"), axis=0, tiled=True),
    )


def gather_feedforward(ffn_gate, ffn_up, ffn_down):
    return (
        lax.all_gather(ffn_gate, ("shard", "ctx"), axis=0, tiled=True),
        lax.all_gather(ffn_up, ("shard", "ctx"), axis=0, tiled=True),
        lax.all_gather(ffn_down, ("shard", "ctx"), axis=0, tiled=True),
    )


def norm_back(grad_normed, normed_hat, inv_scale, gain):
    grad_hat = grad_normed * gain
    inner = jnp.mean(grad_hat * normed_hat, axis=1, keepdims=True)
    return (inv_scale * (grad_hat - normed_hat * inner), jnp.sum(grad_normed * normed_hat, axis=0))


def on_device(
    inputs,
    lengths,
    rec_proj,
    gate_proj,
    out_proj,
    ffn_gate,
    ffn_up,
    ffn_down,
    conv_weight,
    conv_bias,
    a_gate,
    i_gate,
    a_bias,
    i_bias,
    lambda_param,
    rec_norm,
    ffn_norm,
    cotangent,
):
    seqs_here, span_len, width_model = inputs.shape
    row_count = seqs_here * span_len
    taps = conv_weight.shape[0]
    blocks_here, block_width, _ = a_gate.shape
    position = lax.axis_index("ctx") * span_len + jnp.arange(span_len, dtype=jnp.int32)
    valid_mask = position[None, :] < lengths[:, None]
    mask_rows = valid_mask.reshape(row_count, 1).astype(jnp.float32)
    rec_weight, gbr_weight, out_weight = gather_recurrent(rec_proj, gate_proj, out_proj)
    flat_in = inputs.reshape(row_count, width_model)
    inv_one = lax.rsqrt(jnp.mean(flat_in * flat_in, axis=1, keepdims=True) + EPSILON)
    hat_one = flat_in * inv_one
    normed_one = hat_one * rec_norm
    branch = matmul(normed_one, rec_weight).reshape(seqs_here, span_len, -1)
    gate_pre = matmul(normed_one, gbr_weight)
    gate_act = gelu_tanh(gate_pre).reshape(seqs_here, span_len, -1)
    left_edges = passed_along(branch[:, span_len - (taps - 1) :, :], "ctx", 1)
    padded_branch = jnp.concatenate([left_edges, branch], axis=1)
    conv_out = jnp.zeros_like(branch) + conv_bias
    for offset in range(taps):
        conv_out = (
            conv_out
            + conv_weight[offset]
            * padded_branch[:, taps - 1 - offset : taps - 1 - offset + span_len]
        )
    blocked = conv_out.reshape(seqs_here, span_len, blocks_here, block_width)
    a_pre = (
        jnp.einsum("stnj,njk->stnk", blocked, a_gate, precision=HIGHEST).reshape(
            seqs_here, span_len, -1
        )
        + a_bias
    )
    i_pre = (
        jnp.einsum("stnj,njk->stnk", blocked, i_gate, precision=HIGHEST).reshape(
            seqs_here, span_len, -1
        )
        + i_bias
    )
    a_rate = jax.nn.sigmoid(a_pre)
    i_rate = jax.nn.sigmoid(i_pre)
    soft_lambda = jax.nn.softplus(-lambda_param)
    log_decay = -DECAY_CONST * a_rate * soft_lambda
    decay_rate = jnp.exp(log_decay)
    scale_in = jnp.sqrt(-jnp.expm1(2.0 * log_decay))
    drive = scale_in * i_rate * conv_out
    cumul_decay, local_state = lax.associative_scan(affine_pair, (decay_rate, drive), axis=1)
    span_pair = (cumul_decay[:, -1], local_state[:, -1])
    identity_pair = (jnp.ones_like(span_pair[0]), jnp.zeros_like(span_pair[1]))
    carry_in = carried_in(span_pair, "ctx", affine_pair, identity_pair, False)[1]
    rec_state = local_state + cumul_decay * carry_in[:, None, :]
    mixed_rows = (rec_state * gate_act).reshape(row_count, -1)
    mix_total = lax.psum(matmul_nt(mixed_rows, out_weight), "tp")
    after_mix = flat_in + mix_total
    fg_weight, fu_weight, fd_weight = gather_feedforward(ffn_gate, ffn_up, ffn_down)
    inv_two = lax.rsqrt(jnp.mean(after_mix * after_mix, axis=1, keepdims=True) + EPSILON)
    hat_two = after_mix * inv_two
    normed_two = hat_two * ffn_norm
    ffn_gate_pre = matmul(normed_two, fg_weight)
    ffn_up_val = matmul(normed_two, fu_weight)
    gelu_gate = gelu_tanh(ffn_gate_pre)
    hidden = gelu_gate * ffn_up_val
    ffn_total = lax.psum(matmul_nt(hidden, fd_weight), "tp")
    result = after_mix + ffn_total
    block_out = (result * mask_rows).reshape(seqs_here, span_len, width_model)
    grad_result = cotangent.reshape(row_count, width_model) * mask_rows
    fg_weight, fu_weight, fd_weight = gather_feedforward(ffn_gate, ffn_up, ffn_down)
    grad_fd = matmul_tn(grad_result, hidden)
    grad_hidden = matmul(grad_result, fd_weight)
    _, gelu_back = jax.vjp(gelu_tanh, ffn_gate_pre)
    grad_ffn_pre = gelu_back(grad_hidden * ffn_up_val)[0]
    grad_up = grad_hidden * gelu_gate
    grad_fg = matmul_tn(normed_two, grad_ffn_pre)
    grad_fu = matmul_tn(normed_two, grad_up)
    grad_normed_two = lax.psum(
        matmul_nt(grad_ffn_pre, fg_weight) + matmul_nt(grad_up, fu_weight), "tp"
    )
    grad_from_two, grad_norm_two = norm_back(grad_normed_two, hat_two, inv_two, ffn_norm)
    grad_after_mix = grad_result + grad_from_two
    rec_weight, gbr_weight, out_weight = gather_recurrent(rec_proj, gate_proj, out_proj)
    grad_out_weight = matmul_tn(grad_after_mix, mixed_rows)
    grad_mixed = matmul(grad_after_mix, out_weight).reshape(seqs_here, span_len, -1)
    grad_state = grad_mixed * gate_act
    grad_gate_act = (grad_mixed * rec_state).reshape(row_count, -1)
    _, branch_gelu_back = jax.vjp(gelu_tanh, gate_pre)
    grad_gate_pre = branch_gelu_back(grad_gate_act)[0]
    next_decay = jnp.concatenate([decay_rate[:, 1:], jnp.ones_like(decay_rate[:, :1])], axis=1)
    suffix_decay, local_adjoint = lax.associative_scan(
        affine_pair, (next_decay, grad_state), axis=1, reverse=True
    )
    back_pair = (decay_rate[:, 0] * suffix_decay[:, 0], decay_rate[:, 0] * local_adjoint[:, 0])
    incoming = carried_in(back_pair, "ctx", affine_pair, identity_pair, True)[1]
    adjoint = local_adjoint + suffix_decay * incoming[:, None, :]
    prev_state = jnp.concatenate([carry_in[:, None, :], rec_state[:, :-1]], axis=1)
    grad_scale = adjoint * i_rate * conv_out
    grad_log = adjoint * prev_state * decay_rate - grad_scale * decay_rate * decay_rate / scale_in
    grad_lambda = jnp.sum(grad_log * (-DECAY_CONST * a_rate), axis=(0, 1)) * -jax.nn.sigmoid(
        -lambda_param
    )
    grad_a_pre = grad_log * (-DECAY_CONST * soft_lambda) * a_rate * (1.0 - a_rate)
    grad_i_pre = adjoint * scale_in * conv_out * i_rate * (1.0 - i_rate)
    grad_a_bias = jnp.sum(grad_a_pre, axis=(0, 1))
    grad_i_bias = jnp.sum(grad_i_pre, axis=(0, 1))
    grad_a_blocks = grad_a_pre.reshape(seqs_here, span_len, blocks_here, block_width)
    grad_i_blocks = grad_i_pre.reshape(seqs_here, span_len, blocks_here, block_width)
    grad_a_gate = jnp.einsum("stnj,stnk->njk", blocked, grad_a_blocks, precision=HIGHEST)
    grad_i_gate = jnp.einsum("stnj,stnk->njk", blocked, grad_i_blocks, precision=HIGHEST)
    gate_back = jnp.einsum("stnk,njk->stnj", grad_a_blocks, a_gate, precision=HIGHEST) + jnp.einsum(
        "stnk,njk->stnj", grad_i_blocks, i_gate, precision=HIGHEST
    )
    grad_conv = adjoint * scale_in * i_rate + gate_back.reshape(seqs_here, span_len, -1)
    grad_conv_bias = jnp.sum(grad_conv, axis=(0, 1))
    grad_conv_weight = jnp.stack(
        [
            jnp.sum(
                grad_conv * padded_branch[:, taps - 1 - offset : taps - 1 - offset + span_len],
                axis=(0, 1),
            )
            for offset in range(taps)
        ],
        axis=0,
    )
    right_edges = passed_along(grad_conv[:, : taps - 1], "ctx", -1)
    padded_grad = jnp.concatenate([grad_conv, right_edges], axis=1)
    grad_branch = jnp.zeros_like(grad_conv)
    for offset in range(taps):
        grad_branch = grad_branch + conv_weight[offset] * padded_grad[:, offset : offset + span_len]
    grad_branch_rows = grad_branch.reshape(row_count, -1)
    grad_rec = matmul_tn(normed_one, grad_branch_rows)
    grad_gbr = matmul_tn(normed_one, grad_gate_pre)
    grad_normed_one = lax.psum(
        matmul_nt(grad_branch_rows, rec_weight) + matmul_nt(grad_gate_pre, gbr_weight), "tp"
    )
    grad_from_one, grad_norm_one = norm_back(grad_normed_one, hat_one, inv_one, rec_norm)
    input_grad = (grad_after_mix + grad_from_one).reshape(seqs_here, span_len, width_model)
    grad_rec_proj, grad_gate_proj, grad_out_proj, grad_ffn_gate, grad_ffn_up, grad_ffn_down = (
        lax.psum_scatter(grad_rec, ("shard", "ctx"), scatter_dimension=0, tiled=True),
        lax.psum_scatter(grad_gbr, ("shard", "ctx"), scatter_dimension=0, tiled=True),
        lax.psum_scatter(grad_out_weight, ("shard", "ctx"), scatter_dimension=0, tiled=True),
        lax.psum_scatter(grad_fg, ("shard", "ctx"), scatter_dimension=0, tiled=True),
        lax.psum_scatter(grad_fu, ("shard", "ctx"), scatter_dimension=0, tiled=True),
        lax.psum_scatter(grad_fd, ("shard", "ctx"), scatter_dimension=0, tiled=True),
    )
    (
        sum_conv_weight,
        sum_conv_bias,
        sum_a_gate,
        sum_i_gate,
        sum_a_bias,
        sum_i_bias,
        sum_lambda,
        sum_norm_one,
        sum_norm_two,
    ) = lax.psum(
        (
            grad_conv_weight,
            grad_conv_bias,
            grad_a_gate,
            grad_i_gate,
            grad_a_bias,
            grad_i_bias,
            grad_lambda,
            grad_norm_one,
            grad_norm_two,
        ),
        ("shard", "ctx"),
    )
    return (
        block_out,
        input_grad,
        grad_rec_proj,
        grad_gate_proj,
        grad_out_proj,
        grad_ffn_gate,
        grad_ffn_up,
        grad_ffn_down,
        sum_conv_weight,
        sum_conv_bias,
        sum_a_gate,
        sum_i_gate,
        sum_a_bias,
        sum_i_bias,
        sum_lambda,
        sum_norm_one,
        sum_norm_two,
    )


def solution(mesh):
    placed = (
        P("shard", "ctx", None),
        P("shard"),
        P(("shard", "ctx"), "tp"),
        P(("shard", "ctx"), "tp"),
        P(("shard", "ctx"), "tp"),
        P(("shard", "ctx"), "tp"),
        P(("shard", "ctx"), "tp"),
        P(("shard", "ctx"), "tp"),
        P(None, "tp"),
        P("tp"),
        P("tp", None, None),
        P("tp", None, None),
        P("tp"),
        P("tp"),
        P("tp"),
        P(),
        P(),
        P("shard", "ctx", None),
    )
    return jax.shard_map(
        on_device,
        mesh=mesh,
        in_specs=placed,
        out_specs=(
            P("shard", "ctx", None),
            P("shard", "ctx", None),
            P(("shard", "ctx"), "tp"),
            P(("shard", "ctx"), "tp"),
            P(("shard", "ctx"), "tp"),
            P(("shard", "ctx"), "tp"),
            P(("shard", "ctx"), "tp"),
            P(("shard", "ctx"), "tp"),
            P(None, "tp"),
            P("tp"),
            P("tp", None, None),
            P("tp", None, None),
            P("tp"),
            P("tp"),
            P("tp"),
            P(),
            P(),
        ),
        check_vma=False,
    )
```

profile of v0, /device:TPU:0, one launch (start us, length us, event | category | flops | bytes accessed | tf_op | source)
XLA Modules:
  0.0 3134.0 jit_solution(4903990075492314754)
XLA Ops:
  15.8 57.6 %all-gather.7.cloned.1.call-done = f32[1536,512]{1,0:T(8,128)} async-done(((f32[192,512]{1,0:T(8,128)}), f32[1536,512]{1,0:T(8,128)}) %all-gather.7.cloned.1.call-update) | async-done | bytes 3145744 | tf_op jit(solution)/shard_map/all_gather | solution.py:60
  73.4 30.8 fusion.11
  109.0 25.7 all-gather.9.cloned.1.call-done
  134.7 25.4 fusion.9
  371.0 16.5 pad.313
  391.5 16.6 pad.291
  455.6 26.0 fusion.76
  484.5 216.8 %all-reduce.98.cloned.1.call-done = f32[2048,1536]{1,0:T(8,128)} async-done(((f32[2048,1536]{1,0:T(8,128)}), f32[2048,1536]{1,0:T(8,128)}) %all-reduce.98.cloned.1.call-update) | async-done | bytes 12582928 | tf_op jit(solution)/shard_map/psum | solution.py:150
  701.3 14.2 multiply_reduce_fusion.4
  715.5 96.9 %all-gather.17.cloned.1.call-done = f32[1536,1152]{1,0:T(8,128)} async-done(((f32[192,1152]{1,0:T(8,128)}), f32[1536,1152]{1,0:T(8,128)}) %all-gather.17.cloned.1.call-update) | async-done | bytes 7077904 | tf_op jit(solution)/shard_map/all_gather | solution.py:70
  812.3 56.0 %fusion.6 = f32[2048,1152]{1,0:T(8,128)} fusion(f32[1536,1152]{1,0:T(8,128)} %all-gather.17.cloned.1.call-done, f32[1,2048,1536]{2,1,0:T(8,128)} %param.35, f32[2048]{0:T(1024)S(1)} %fusion.106), kind=kOutput, calls=%fused_computation.20 | convolution fusion | flops 43489689600 | bytes 29106176 | tf_op jit(solution)/shard_map/dot_general | solution.py:39
  868.4 53.0 %all-gather.15.cloned.1.call-done = f32[1536,1152]{1,0:T(8,128)} async-done(((f32[192,1152]{1,0:T(8,128)}), f32[1536,1152]{1,0:T(8,128)}) %all-gather.15.cloned.1.call-update) | async-done | bytes 7077904 | tf_op jit(solution)/shard_map/all_gather | solution.py:69
  921.4 57.0 %fusion.17 = f32[2048,1152]{1,0:T(8,128)} fusion(f32[1536,1152]{1,0:T(8,128)} %all-gather.15.cloned.1.call-done, f32[2048,1536]{1,0:T(8,128)} %get-tuple-element.82, f32[1536]{0:T(1024)S(1)} %copy-done.59, f32[2048]{0:T(1024)S(1)} %add_rsqrt_fusion), kind=kOutput, calls=%fused_computation.31 | convolution fusion | flops 43492835328 | bytes 29112320 | tf_op jit(solution)/shard_map/dot_general | solution.py:39
  978.4 52.2 %all-gather.13.cloned.1.call-done = f32[1536,1152]{1,0:T(8,128)} async-done(((f32[192,1152]{1,0:T(8,128)}), f32[1536,1152]{1,0:T(8,128)}) %all-gather.13.cloned.1.call-update) | async-done | bytes 7077904 | tf_op jit(solution)/shard_map/all_gather | solution.py:68
  1030.6 65.7 %fusion.26 = (f32[2048,1152]{1,0:T(8,128)}, f32[2048,1152]{1,0:T(8,128)}) fusion(f32[2048,1152]{1,0:T(8,128)} %fusion.6, f32[2048,1152]{1,0:T(8,128)} %fusion.17, f32[1536,1152]{1,0:T(8,128)} %all-gather.13.cloned.1.call-done, f32[2048,1536]{1,0:T(8,128)} %get-tuple-element.82, f32[1536]{0:T(1024)S(1)} %copy-done.59, f32[2048]{0:T(1024)S(1)} %add_rsqrt_fusion), kind=kOutput, calls=%fused_computation.40 | convolution fusion | flops 43540021248 | bytes 57423872 | tf_op jit(solution)/shard_map/dot_general | solution.py:39
  1096.3 54.7 %fusion.142 = f32[2048,1536]{1,0:T(8,128)} fusion(f32[2048,1152]{1,0:T(8,128)} %get-tuple-element.185, f32[1536,1152]{1,0:T(8,128)S(1)} %copy-done.89), kind=kOutput, calls=%fused_computation.315 | convolution fusion | flops 43486543872 | bytes 29097984 | tf_op jit(solution)/shard_map/dot_general | solution.py:43
  1151.0 57.8 %convolution_add_fusion.1 = f32[2048,1536]{1,0:T(8,128)} fusion(f32[2048,1536]{1,0:T(8,128)} %fusion.142, f32[1536,1152]{1,0:T(8,128)S(1)} %copy-done.88, f32[2048,1152]{1,0:T(8,128)} %fusion.6, f32[2048,1152]{1,0:T(8,128)} %get-tuple-element.186), kind=kOutput, calls=%fused_computation.47 | convolution fusion | flops 43510923264 | bytes 51118080 | tf_op jit(solution)/shard_map/dot_general | solution.py:43
  1246.8 16.8 slice.855
  1263.5 17.3 slice.846
  1291.3 136.5 %all-reduce.100.cloned.1.call-done = f32[2048,1536]{1,0:T(8,128)} async-done(((f32[2048,1536]{1,0:T(8,128)}), f32[2048,1536]{1,0:T(8,128)}) %all-reduce.100.cloned.1.call-update) | async-done | bytes 12582928 | tf_op jit(solution)/shard_map/psum | solution.py:172
  1439.7 15.5 multiply_add_fusion
  1455.2 22.9 fusion.143
  1514.6 16.6 slice.850
  1666.5 16.5 pad.334
  1692.0 16.8 pad.357
  1728.3 32.6 %rev.5 = f32[1,2048,512]{2,1,0:T(8,128)} reverse(f32[1,2048,512]{2,1,0:T(8,128)} %add.847), dimensions={1} | reverse | bytes 8388608 | tf_op jit(solution)/shard_map/rev | solution.py:185
  1760.9 32.5 %rev.4 = f32[1,2048,512]{2,1,0:T(8,128)} reverse(f32[1,2048,512]{2,1,0:T(8,128)} %add.836), dimensions={1} | reverse | bytes 8388608 | tf_op jit(solution)/shard_map/rev | solution.py:185
  1802.2 12.3 multiply_reduce_fusion.5
  1855.9 16.2 multiply_reduce_fusion.8
  1873.5 58.9 %fusion.117 = f32[2048,1536]{1,0:T(8,128)} fusion(f32[1536,1152]{1,0:T(8,128)} %all-gather.17.cloned.1.call-done, f32[2048,1152]{1,0:T(8,128)} %fusion.17, f32[2048,1152]{1,0:T(8,128)} %get-tuple-element.186), kind=kOutput, calls=%fused_computation.296 | convolution fusion | flops 43507777536 | bytes 38535168 | tf_op jit(solution)/shard_map/dot_general | solution.py:43
  1937.0 21.9 fusion.144
  1958.9 32.5 %convolution_add_fusion = f32[2048,1536]{1,0:T(8,128)} fusion(f32[2048,1536]{1,0:T(8,128)S(1)} %fusion.144, f32[1536,512]{1,0:T(8,128)} %all-gather.9.cloned.1.call-done, f32[2048,512]{1,0:T(8,128)S(1)} %copy-done.9, f32[1,2048,512]{2,1,0:T(8,128)S(1)} %copy-done.5, f32[2048,512]{1,0:T(8,128)S(1)} %copy-done.18), kind=kOutput, calls=%fused_computation.42 | convolution fusion | flops 19351470080 | bytes 40894464 | tf_op jit(solution)/shard_map/dot_general | solution.py:43
  2005.5 29.6 fusion.7
  2035.4 25.7 fusion.74
  2061.5 26.3 fusion
  2088.5 58.1 %fusion.15 = f32[1536,1152]{1,0:T(8,128)} fusion(f32[2048,1152]{1,0:T(8,128)} %get-tuple-element.185, f32[2048,1536]{1,0:T(8,128)} %get-tuple-element.82, f32[1536]{0:T(1024)S(1)} %copy-done.60, f32[2048]{0:T(1024)S(1)} %copy-done.53), kind=kOutput, calls=%fused_computation.29 | convolution fusion | flops 43492835328 | bytes 29112320 | tf_op jit(solution)/shard_map/dot_general | solution.py:49
  2146.8 61.1 %fusion.13 = f32[1536,1152]{1,0:T(8,128)} fusion(f32[2048,1536]{1,0:T(8,128)} %get-tuple-element.82, f32[1536]{0:T(1024)S(1)} %copy-done.60, f32[2048]{0:T(1024)S(1)} %copy-done.53, f32[2048,1152]{1,0:T(8,128)} %fusion.6, f32[2048,1152]{1,0:T(8,128)} %get-tuple-element.186), kind=kOutput, calls=%fused_computation.27 | convolution fusion | flops 43514068992 | bytes 38549504 | tf_op jit(solution)/shard_map/dot_general | solution.py:49
  2208.6 61.0 %fusion.5 = f32[1536,1152]{1,0:T(8,128)} fusion(f32[1,2048,1536]{2,1,0:T(8,128)} %param.35, f32[2048]{0:T(1024)S(1)} %copy-done.51, f32[2048,1152]{1,0:T(8,128)} %fusion.17, f32[2048,1152]{1,0:T(8,128)} %get-tuple-element.186), kind=kOutput, calls=%fused_computation.19 | convolution fusion | flops 43510923264 | bytes 38543360 | tf_op jit(solution)/shard_map/dot_general | solution.py:49
  2270.4 146.2 %all-reduce.104.cloned.1.call-done = (f32[2048,1536]{1,0:T(8,128)}, f32[2048,1536]{1,0:T(8,128)}) async-done(((f32[2048,1536]{1,0:T(8,128)}, f32[2048,1536]{1,0:T(8,128)}), (f32[2048,1536]{1,0:T(8,128)}, f32[2048,1536]{1,0:T(8,128)})) %all-reduce.104.cloned.1.call-update) | async-done | bytes 25165840 | tf_op jit(solution)/shard_map/psum | solution.py:160
  2426.3 37.8 %all-reduce.90 = (f32[4,512]{1,0:T(4,128)}, f32[512]{0:T(512)}, f32[512]{0:T(512)}, f32[512]{0:T(512)}, f32[512]{0:T(512)}, /*index=5*/f32[1536]{0:T(1024)}, f32[1536]{0:T(1024)}) all-reduce(f32[4,512]{1,0:T(4,128)S(1)} %pad_maximum_fusion.37, f32[512]{0:T(512)S(1)} %copy-done.82, ...), channel_id=1, replica_groups=mesh['shard'=4,'ctx'=2,'tp'=4] {'shard','ctx'}, use_global_device_ids=true, to_apply=%region_18.19 | all-reduce | flops 7168 | bytes 57344 | tf_op jit(solution)/shard_map/psum | solution.py:251
  2464.1 14.3 multiply_bitcast_fusion
  2480.5 14.5 add_bitcast_fusion
  2495.0 76.4 %reduce-scatter.9.cloned.1.call-done = f32[192,512]{1,0:T(8,128)} async-done(((f32[1536,512]{1,0:T(8,128)}), f32[192,512]{1,0:T(8,128)}) %reduce-scatter.9.cloned.1.call-update) | async-done | bytes 393232 | tf_op jit(solution)/shard_map/reduce_scatter | solution.py:235
  2571.4 77.6 %reduce-scatter.11.cloned.1.call-done = f32[192,512]{1,0:T(8,128)} async-done(((f32[1536,512]{1,0:T(8,128)}), f32[192,512]{1,0:T(8,128)}) %reduce-scatter.11.cloned.1.call-update) | async-done | bytes 393232 | tf_op jit(solution)/shard_map/reduce_scatter | solution.py:236
  2649.0 77.7 %reduce-scatter.7.cloned.1.call-done = f32[192,512]{1,0:T(8,128)} async-done(((f32[1536,512]{1,0:T(8,128)}), f32[192,512]{1,0:T(8,128)}) %reduce-scatter.7.cloned.1.call-update) | async-done | bytes 393232 | tf_op jit(solution)/shard_map/reduce_scatter | solution.py:234
  2726.7 132.3 %reduce-scatter.13.cloned.1.call-done = f32[192,1152]{1,0:T(8,128)} async-done(((f32[1536,1152]{1,0:T(8,128)}), f32[192,1152]{1,0:T(8,128)}) %reduce-scatter.13.cloned.1.call-update) | async-done | bytes 884752 | tf_op jit(solution)/shard_map/reduce_scatter | solution.py:237
  2859.0 132.7 %reduce-scatter.15.cloned.1.call-done = f32[192,1152]{1,0:T(8,128)} async-done(((f32[1536,1152]{1,0:T(8,128)}), f32[192,1152]{1,0:T(8,128)}) %reduce-scatter.15.cloned.1.call-update) | async-done | bytes 884752 | tf_op jit(solution)/shard_map/reduce_scatter | solution.py:238
  2991.7 132.2 %reduce-scatter.17.cloned.1.call-done = f32[192,1152]{1,0:T(8,128)} async-done(((f32[1536,1152]{1,0:T(8,128)}), f32[192,1152]{1,0:T(8,128)}) %reduce-scatter.17.cloned.1.call-update) | async-done | bytes 884752 | tf_op jit(solution)/shard_map/reduce_scatter | solution.py:239
  (615 shorter events, 624.6 us)
Async XLA Ops:
  7.2 161.7 %copy-start = (f32[4,128,128]{2,1,0:T(8,128)S(1)}, f32[4,128,128]{2,1,0:T(8,128)}, u32[]{:S(2)}) copy-start(f32[4,128,128]{2,1,0:T(8,128)} %param.29) | copy-start | bytes 786436
  7.2 66.2 %all-gather.7.cloned.1.call-start = ((), (), s32[]{:S(2)}) async-start(), calls=%async_computation.6 | async-start | bytes 3538944 | tf_op jit(solution)/shard_map/all_gather | solution.py:60
  7.9 126.8 %all-gather.9.cloned.1.call-start = ((), (), s32[]{:S(2)}) async-start(), calls=%async_computation.7 | async-start | bytes 3538944 | tf_op jit(solution)/shard_map/all_gather | solution.py:61
  8.7 446.9 %all-gather.11.cloned.1.call-start = ((), (), s32[]{:S(2)}) async-start(), calls=%async_computation.8 | async-start | bytes 3538944 | tf_op jit(solution)/shard_map/all_gather | solution.py:62
  9.4 691.8 %all-reduce.98.cloned.1.call-start = ((), (), s32[]{:S(2)}) async-start(), calls=%async_computation.9 | async-start | bytes 25165824 | tf_op jit(solution)/shard_map/psum | solution.py:150
  10.2 185.9 %copy-start.54 = (f32[512]{0:T(512)}, f32[512]{0:T(512)S(1)}, u32[]{:S(2)}) copy-start(f32[512]{0:T(512)S(1)} %fusion.115) | copy-start | bytes 6148
  10.2 63.2 %copy-start.56 = (f32[1536]{0:T(1024)S(1)}, f32[1536]{0:T(1024)}, u32[]{:S(2)}) copy-start(f32[1536]{0:T(1024)} %param.33) | copy-start | bytes 18436
  15.7 119.0 %copy-start.48 = (f32[2048]{0:T(1024)}, f32[2048]{0:T(1024)S(1)}, u32[]{:S(2)}) copy-start(f32[2048]{0:T(1024)S(1)} %add_rsqrt_fusion.1) | copy-start | bytes 24580
  15.7 144.4 %copy-start.69 = (f32[1,512]{1,0:T(1,128)}, f32[1,512]{1,0:T(1,128)S(1)}, u32[]{:S(2)}) copy-start(f32[1,512]{1,0:T(1,128)S(1)} %get-tuple-element.169) | copy-start | bytes 6148
  15.7 144.4 %copy-start.71 = (f32[1,512]{1,0:T(1,128)}, f32[1,512]{1,0:T(1,128)S(1)}, u32[]{:S(2)}) copy-start(f32[1,512]{1,0:T(1,128)S(1)} %get-tuple-element.170) | copy-start | bytes 6148
  15.8 144.4 %copy-start.73 = (f32[1,512]{1,0:T(1,128)}, f32[1,512]{1,0:T(1,128)S(1)}, u32[]{:S(2)}) copy-start(f32[1,512]{1,0:T(1,128)S(1)} %get-tuple-element.171) | copy-start | bytes 6148
  15.8 144.4 %copy-start.75 = (f32[1,512]{1,0:T(1,128)}, f32[1,512]{1,0:T(1,128)S(1)}, u32[]{:S(2)}) copy-start(f32[1,512]{1,0:T(1,128)S(1)} %get-tuple-element.172) | copy-start | bytes 6148
  106.2 53.9 %copy-start.87 = (f32[512]{0:T(512)S(1)}, f32[512]{0:T(512)}, u32[]{:S(2)}) copy-start(f32[512]{0:T(512)} %param.27) | copy-start | bytes 6148
  106.2 53.9 %collective-permute-start = (f32[1,3,512]{2,1,0:T(4,128)S(1)}, f32[1,3,512]{2,1,0:T(4,128)S(1)}, u32[]{:S(2)}, u32[]{:S(2)}) collective-permute-start(f32[1,3,512]{2,1,0:T(4,128)S(1)} %slice.960), channel_id=1, source_target_pairs={{0,4},{1,5},{2,6},{3,7},{8,12},{9,13},{10,14},{11,15},{16,20},{17,... | collective-permute-start | bytes 18440 | tf_op jit(solution)/shard_map/ppermute | solution.py:14
  134.7 25.4 copy-start.7
  343.1 19.7 copy-start.32
  481.6 330.7 %all-gather.17.cloned.1.call-start = ((), (), s32[]{:S(2)}) async-start(), calls=%async_computation.12 | async-start | bytes 7962624 | tf_op jit(solution)/shard_map/all_gather | solution.py:70
  482.2 439.2 %all-gather.15.cloned.1.call-start = ((), (), s32[]{:S(2)}) async-start(), calls=%async_computation.11 | async-start | bytes 7962624 | tf_op jit(solution)/shard_map/all_gather | solution.py:69
  482.8 547.8 %all-gather.13.cloned.1.call-start = ((), (), s32[]{:S(2)}) async-start(), calls=%async_computation.10 | async-start | bytes 7962624 | tf_op jit(solution)/shard_map/all_gather | solution.py:68
  483.5 944.3 %all-reduce.100.cloned.1.call-start = ((), (), s32[]{:S(2)}) async-start(), calls=%async_computation.13 | async-start | bytes 25165824 | tf_op jit(solution)/shard_map/psum | solution.py:172
  484.5 953.7 %copy-start.50 = (f32[2048]{0:T(1024)}, f32[2048]{0:T(1024)S(1)}, u32[]{:S(2)}) copy-start(f32[2048]{0:T(1024)S(1)} %fusion.106) | copy-start | bytes 24580
  715.4 722.7 %copy-start.52 = (f32[2048]{0:T(1024)}, f32[2048]{0:T(1024)S(1)}, u32[]{:S(2)}) copy-start(f32[2048]{0:T(1024)S(1)} %add_rsqrt_fusion) | copy-start | bytes 24580
  715.5 205.9 %copy-start.59 = (f32[1536]{0:T(1024)S(1)}, f32[1536]{0:T(1024)}, u32[]{:S(2)}) copy-start(f32[1536]{0:T(1024)} %param.34) | copy-start | bytes 18436
  1030.6 65.7 %copy-start.89 = (f32[1536,1152]{1,0:T(8,128)S(1)}, f32[1536,1152]{1,0:T(8,128)}, u32[]{:S(2)}) copy-start(f32[1536,1152]{1,0:T(8,128)} %all-gather.13.cloned.1.call-done) | copy-start | bytes 21233668
  1096.3 54.7 %copy-start.88 = (f32[1536,1152]{1,0:T(8,128)S(1)}, f32[1536,1152]{1,0:T(8,128)}, u32[]{:S(2)}) copy-start(f32[1536,1152]{1,0:T(8,128)} %all-gather.15.cloned.1.call-done) | copy-start | bytes 21233668
  1208.8 1207.8 %all-reduce.104.cloned.1.call-start = ((), (), s32[]{:S(2)}) async-start(), calls=%async_computation.21 | async-start | bytes 50331648 | tf_op jit(solution)/shard_map/psum | solution.py:160
  1455.2 22.9 copy-start.8
  1760.9 41.2 %copy-start.55 = (f32[512]{0:T(512)S(1)}, f32[512]{0:T(512)}, u32[]{:S(2)}) copy-start(f32[512]{0:T(512)} %copy-done.54) | copy-start | bytes 6148
  1760.9 41.2 %copy-start.64 = (f32[512]{0:T(512)S(1)}, f32[512]{0:T(512)}, u32[]{:S(2)}) copy-start(f32[512]{0:T(512)} %param.31) | copy-start | bytes 6148
  1760.9 41.2 %copy-start.66 = (f32[512]{0:T(512)S(1)}, f32[512]{0:T(512)}, u32[]{:S(2)}) copy-start(f32[512]{0:T(512)} %param.30) | copy-start | bytes 6148
  1760.9 41.2 %copy-start.68 = (f32[1,1,512]{2,1,0:T(1,128)S(1)}, f32[1,1,512]{2,1,0:T(1,128)}, u32[]{:S(2)}) copy-start(f32[1,1,512]{2,1,0:T(1,128)} %copy-done.67) | copy-start | bytes 6148
  1872.2 60.3 %copy-start.70 = (f32[1,512]{1,0:T(1,128)S(1)}, f32[1,512]{1,0:T(1,128)}, u32[]{:S(2)}) copy-start(f32[1,512]{1,0:T(1,128)} %copy-done.69) | copy-start | bytes 6148
  1872.2 60.3 %copy-start.72 = (f32[1,512]{1,0:T(1,128)S(1)}, f32[1,512]{1,0:T(1,128)}, u32[]{:S(2)}) copy-start(f32[1,512]{1,0:T(1,128)} %copy-done.71) | copy-start | bytes 6148
  1872.2 60.3 %copy-start.74 = (f32[1,512]{1,0:T(1,128)S(1)}, f32[1,512]{1,0:T(1,128)}, u32[]{:S(2)}) copy-start(f32[1,512]{1,0:T(1,128)} %copy-done.73) | copy-start | bytes 6148
  1872.2 60.3 %copy-start.76 = (f32[1,512]{1,0:T(1,128)S(1)}, f32[1,512]{1,0:T(1,128)}, u32[]{:S(2)}) copy-start(f32[1,512]{1,0:T(1,128)} %copy-done.75) | copy-start | bytes 6148
  1872.2 60.3 %collective-permute-start.1 = (f32[1,3,512]{2,1,0:T(4,128)S(1)}, f32[1,3,512]{2,1,0:T(4,128)S(1)}, u32[]{:S(2)}, u32[]{:S(2)}) collective-permute-start(f32[1,3,512]{2,1,0:T(4,128)S(1)} %slice.1106), channel_id=1, source_target_pairs={{4,0},{5,1},{6,2},{7,3},{12,8},{13,9},{14,10},{15,11},{20,16},{21,... | collective-permute-start | bytes 18440 | tf_op jit(solution)/shard_map/ppermute | solution.py:14
  1937.0 21.9 copy-start.5
  1937.0 22.0 copy-start.9
  1937.0 22.0 copy-start.18
  1991.5 503.6 %all-reduce.102.cloned.1.call-start = ((), (), s32[]{:S(2)}) async-start(), calls=%async_computation.20 | async-start | bytes 1048576 | tf_op jit(solution)/shard_map/psum | solution.py:251
  2005.2 566.2 %reduce-scatter.9.cloned.1.call-start = ((), (), s32[]{:S(2)}) async-start(), calls=%async_computation.15 | async-start | bytes 3538944 | tf_op jit(solution)/shard_map/reduce_scatter | solution.py:235
  2035.1 613.9 %reduce-scatter.11.cloned.1.call-start = ((), (), s32[]{:S(2)}) async-start(), calls=%async_computation.16 | async-start | bytes 3538944 | tf_op jit(solution)/shard_map/reduce_scatter | solution.py:236
  2061.2 27.3 copy-start.53
  2061.2 27.3 copy-start.60
  2061.2 665.5 %reduce-scatter.7.cloned.1.call-start = ((), (), s32[]{:S(2)}) async-start(), calls=%async_computation.14 | async-start | bytes 3538944 | tf_op jit(solution)/shard_map/reduce_scatter | solution.py:234
  2087.9 771.1 %reduce-scatter.13.cloned.1.call-start = ((), (), s32[]{:S(2)}) async-start(), calls=%async_computation.17 | async-start | bytes 7962624 | tf_op jit(solution)/shard_map/reduce_scatter | solution.py:237
  2146.6 845.0 %reduce-scatter.15.cloned.1.call-start = ((), (), s32[]{:S(2)}) async-start(), calls=%async_computation.18 | async-start | bytes 7962624 | tf_op jit(solution)/shard_map/reduce_scatter | solution.py:238
  2207.9 916.0 %reduce-scatter.17.cloned.1.call-start = ((), (), s32[]{:S(2)}) async-start(), calls=%async_computation.19 | async-start | bytes 7962624 | tf_op jit(solution)/shard_map/reduce_scatter | solution.py:239
  (60 other events, 326.3 us)
Sparse Core Ops, SparseCore 0:
  10.2 63.1 all-gather.6
  75.6 59.0 all-gather.8
  136.9 59.2 all-gather.10
  481.7 219.4 all-reduce.97
  703.3 108.9 all-gather.16
  814.4 106.9 all-gather.14
  923.6 106.9 all-gather.12
  1208.9 218.8 all-reduce.99
  1991.6 424.9 all-reduce.103
  2420.9 72.8 all-reduce.101
  2497.9 73.4 reduce-scatter.8
  2575.4 73.5 reduce-scatter.10
  2653.2 73.5 reduce-scatter.6
  2730.8 128.1 reduce-scatter.12
  2863.5 128.0 reduce-scatter.14
  2995.8 128.0 reduce-scatter.16
where the time goes:
time: 3150 us; the launch traced here: 3130 us
  waiting for transfers between devices  1420 us (45%)
  matrix products  818 us (26%)
  local copies, waits for them, and re-layouts  589 us (19%)
  other arithmetic  230 us (7%)
  blocking collectives  55.2 us (2%)
    dot_general x6, matrix products, matmul_tn(): lax.dot_general(left, right, (((0,), (0,)), ((), ())), precision=HIGHEST,...  262 us
    dot_general x6, matrix products, matmul(): jnp.dot(left, right, precision=HIGHEST, preferred_element_type=jnp.float32)  258 us
    dot_general x6, matrix products, matmul_nt(): lax.dot_general(left, right, (((1,), (1,)), ((), ())), precision=HIGHEST,...  252 us
    psum x1, waiting for transfers between devices, on_device(): mix_total = lax.psum(matmul_nt(mixed_rows, out_weight), 'tp')  217 us
    slice x81, local copies, waits for them, and re-layouts, on_device(): lax.associative_scan(affine_pair, (next_decay, grad_state), axis=1, rever...  193 us
    psum x1, waiting for transfers between devices, on_device(): ffn_total = lax.psum(matmul_nt(hidden, fd_weight), 'tp')  146 us
    psum x1, waiting for transfers between devices, on_device(): lax.psum(matmul_nt(grad_ffn_pre, fg_weight) + matmul_nt(grad_up, fu_weigh...  136 us
    reduce_scatter x1, waiting for transfers between devices, on_device(): lax.psum_scatter(grad_fu, ('shard', 'ctx'), scatter_dimension=0, tiled=True)  133 us
  transfers between devices with their start and end apart: 18, of which 14 were waited for; matrix products, arithmetic and copies ran while one was open for 30% of the time, Pallas kernels for 0%

commit v1 on v0

v1 whole, which is shorter than its diff:
```python
import functools

import jax
import jax.numpy as jnp
from jax import lax
from jax.experimental import pallas as pl
from jax.experimental.pallas import tpu as pltpu
from jax.sharding import PartitionSpec as P

HIGH = lax.Precision.HIGH
EPSILON = 1e-06
DECAY_CONST = 8.0
ROOT = 0.7978845608028654
CUBIC = 0.044715
F32 = jnp.float32
BF16 = jnp.bfloat16
VMEM_BYTES = 56 * 1024 * 1024


def matmul(left, right):
    return jnp.dot(left, right, precision=HIGH, preferred_element_type=F32)


def matmul_nt(left, right):
    return lax.dot_general(
        left, right, (((1,), (1,)), ((), ())), precision=HIGH, preferred_element_type=F32
    )


def matmul_tn(left, right):
    return lax.dot_general(
        left, right, (((0,), (0,)), ((), ())), precision=HIGH, preferred_element_type=F32
    )


def halves(values):
    high = values.astype(BF16)
    return high, (values - high.astype(F32)).astype(BF16)


def three_pass(left, right, dims):
    left_high, left_low = halves(left)
    right_high, right_low = halves(right)

    def part(one, two):
        return lax.dot_general(one, two, (dims, ((), ())), preferred_element_type=F32)

    return part(left_high, right_high) + (part(left_high, right_low) + part(left_low, right_high))


def gelu_parts(values):
    square = values * values
    curve = jnp.tanh(ROOT * values * (1.0 + CUBIC * square))
    act = 0.5 * values * (1.0 + curve)
    slope = 0.5 * (1.0 + curve) + 0.5 * values * (1.0 - curve * curve) * ROOT * (
        1.0 + 3.0 * CUBIC * square
    )
    return act, slope


def gelu(values):
    return 0.5 * values * (1.0 + jnp.tanh(ROOT * values * (1.0 + CUBIC * values * values)))


def expm1_negative(values):
    series = jnp.full_like(values, 1.0)
    for order in range(11, 1, -1):
        series = 1.0 + values * (1.0 / order) * series
    return jnp.where(values > -1.0, values * series, jnp.exp(values) - 1.0)


def decay_parts(a_rate, soft_lambda):
    log_decay = -DECAY_CONST * a_rate * soft_lambda
    return jnp.exp(log_decay), jnp.sqrt(-expm1_negative(2.0 * log_decay))


def passed_along(block, axis, distance):
    devices = range(lax.axis_size(axis))
    route = [(i - distance, i) for i in devices if i - distance in devices]
    return lax.ppermute(block, axis, route)


def rotated(block, axis, distance):
    count = lax.axis_size(axis)
    return lax.ppermute(block, axis, [(i, (i + distance) % count) for i in range(count)])


def swapped(block, axis, bit):
    return lax.ppermute(block, axis, [(i, i ^ bit) for i in range(lax.axis_size(axis))])


def carried_in(decay, state, sign):
    count = lax.axis_size("ctx")
    mine = lax.axis_index("ctx")
    place = mine if sign > 0 else count - 1 - mine
    distance = 1
    while distance < count - 1:
        earlier_decay = passed_along(decay, "ctx", sign * distance)
        earlier_state = passed_along(state, "ctx", sign * distance)
        has = place >= distance
        state = jnp.where(has, decay * earlier_state + state, state)
        decay = jnp.where(has, decay * earlier_decay, decay)
        distance *= 2
    return passed_along(state, "ctx", sign)


class Box:
    def __init__(self, v):
        self.v = v


class Sequence:
    def __init__(self):
        self.pending = []

    def gate(self, *values):
        boxes = list({id(b): b for b in [*self.pending, *values] if isinstance(b, Box)}.values())
        raw = [value for value in values if not isinstance(value, Box)]
        held, raw = lax.optimization_barrier(([b.v for b in boxes], raw))
        for box, value in zip(boxes, held):
            box.v = value
        raw = iter(raw)
        return [value.v if isinstance(value, Box) else next(raw) for value in values]

    def wait(self, *boxes):
        self.pending = [*self.pending, *boxes]

    def step(self, function, *values):
        out = function(*self.gate(*values))
        if isinstance(out, (tuple, list)):
            out = [Box(value) for value in out]
            self.pending = list(out)
        else:
            out = Box(out)
            self.pending = [out]
        return out

    def send(self, move, value, *args):
        return Box(move(self.gate(value)[0], *args))


class Gather:
    def __init__(self, block, order):
        self.rows, self.width = block.shape
        self.shards = lax.axis_size("shard")
        self.z, self.x = lax.axis_index("shard"), lax.axis_index("ctx")
        self.order = order
        self.own, self.other = [Box(block)], []
        self.pairs = []

    def swap(self):
        self.other.append(self.order.send(swapped, self.own[len(self.other)], "ctx", 1))
        return self.other[-1]

    def turn(self):
        self.own.append(self.order.send(rotated, self.own[-1], "shard", 1))
        return self.own[-1]

    def turn_pair(self):
        if not self.pairs:
            self.pairs.append(
                self.order.step(lambda one, two: jnp.stack([one, two]), self.own[0], self.other[0])
            )
        self.pairs.append(self.order.send(rotated, self.pairs[-1], "shard", 1))
        return self.pairs[-1]

    def whole(self):
        whole = jnp.zeros((self.shards, 2, self.rows, self.width), F32)

        def put(whole, piece, step, span):
            owner = (self.z - step) % self.shards
            piece = piece.reshape(1, -1, self.rows, self.width)
            return lax.dynamic_update_slice(whole, piece, (owner, span, 0, 0))

        for step in range(self.shards):
            own, other = (
                self.pairs[step].v if self.pairs else (self.own[step].v, self.other[step].v)
            )
            whole = put(put(whole, own, step, self.x), other, step, 1 - self.x)
        return Box(whole.reshape(-1, self.width))


def gather_plain(block):
    return lax.all_gather(block, ("shard", "ctx"), axis=0, tiled=True)


def over_shard(rows):
    shards, count, width = rows.shape
    return lax.psum_scatter(
        rows.reshape(shards * count, width), "shard", scatter_dimension=0, tiled=True
    )


class Scatter:
    def __init__(self, kept, sent, order, earlier):
        self.kept, self.sent, self.order, self.earlier = kept, sent, order, earlier
        self.rows = kept.v.shape[1]

    def start_ctx(self):
        self.arriving = self.order.send(swapped, self.sent, "ctx", 1)

    def take_turn(self):
        if self.earlier:
            self.order.wait(self.earlier[-1])

    def end_ctx(self):
        self.take_turn()
        both = self.order.step(lambda one, two: one + two, self.kept, self.arriving)
        self.result = Box(over_shard(self.order.gate(both)[0]))
        self.earlier.append(self.result)

    def start_shard(self):
        self.take_turn()
        both = self.order.step(
            lambda one, two: jnp.concatenate([one, two], axis=1), self.kept, self.sent
        )
        self.both = Box(over_shard(self.order.gate(both)[0]))
        self.earlier.append(self.both)

    def end_shard(self):
        rows = self.rows
        sent = self.order.step(lambda both: both[rows:], self.both)
        self.arriving = self.order.send(swapped, sent, "ctx", 1)
        self.result = self.order.step(
            lambda both, other: both[:rows] + other, self.both, self.arriving
        )


def scatter_plain(total):
    return lax.psum_scatter(total, ("shard", "ctx"), scatter_dimension=0, tiled=True)


class TpSum:
    def __init__(self, kept, sent, order):
        self.order, self.kept, self.arrived = order, kept, None
        self.levels = lax.axis_size("tp") == 4
        if self.levels:
            self.arriving = order.send(swapped, sent, "tp", 1)
        else:
            self.kept = Box(lax.psum(kept.v, "tp"))
            self.arriving = Box(lax.psum(sent.v, "tp"))

    def cross(self):
        if self.levels:
            self.kept = self.order.step(lambda one, two: one + two, self.kept, self.arriving)
            self.arriving = self.order.send(swapped, self.kept, "tp", 2)

    def share(self):
        if self.levels:
            self.kept = self.order.step(lambda one, two: one + two, self.kept, self.arriving)
            self.arriving = self.order.send(swapped, self.kept, "tp", 1)

    def rows(self, kept, arriving):
        first = lax.axis_index("tp") % 2 == 0
        low = jnp.where(first, kept, arriving)
        high = jnp.where(first, arriving, kept)
        return jnp.concatenate([low, high], axis=0)


class SmallSum:
    def __init__(self, value, order, axes):
        self.value, self.order, self.arriving = value, order, None
        self.bits = []
        if any(lax.axis_size(axis) & (lax.axis_size(axis) - 1) for axis in axes):
            self.value = Box(lax.psum(value.v, axes))
            return
        for axis in axes:
            bit = 1
            while bit < lax.axis_size(axis):
                self.bits.append((axis, bit))
                bit *= 2

    def advance(self):
        if self.arriving is not None:
            self.value = self.order.step(lambda one, two: one + two, self.value, self.arriving)
            self.arriving = None
        if self.bits:
            self.arriving = self.order.send(swapped, self.value, *self.bits.pop(0))
            return True
        return False


def row_of(table, index):
    return table[index : index + 1, :]


def tile_scan(decay, value, reverse):
    rows, width = decay.shape
    decay = decay.reshape(rows // 8, 8, width)
    value = value.reshape(rows // 8, 8, width)
    place = lax.broadcasted_iota(jnp.int32, decay.shape, 1)
    for step in (1, 2, 4):
        shift = 8 - step if reverse else step
        inside = place < 8 - step if reverse else place >= step
        other_decay = jnp.where(inside, pltpu.roll(decay, shift, 1), 1.0)
        other_value = jnp.where(inside, pltpu.roll(value, shift, 1), 0.0)
        value = value + decay * other_value
        decay = decay * other_decay
    return decay.reshape(rows, width), value.reshape(rows, width)


def chain_tiles(decay_ref, value_ref, decay_carry, value_carry, reverse):
    tiles = decay_ref.shape[0] // 8
    edge = 0 if reverse else 7
    for step in range(tiles):
        tile = tiles - 1 - step if reverse else step
        rows = slice(tile * 8, tile * 8 + 8)
        decay, value = decay_ref[rows, :], value_ref[rows, :]
        value = value + decay * value_carry
        decay = decay * decay_carry
        decay_ref[rows, :], value_ref[rows, :] = decay, value
        decay_carry = jnp.broadcast_to(decay[edge : edge + 1, :], decay.shape)
        value_carry = jnp.broadcast_to(value[edge : edge + 1, :], value.shape)
    return decay_carry, value_carry


def forward_kernel(
    branch_ref, edge_ref, taps_ref, table_ref, gate_ref,
    conv_ref, a_ref, i_ref, cumul_ref, state_ref, pair_ref,
    padded, carry,
):
    rows, width = branch_ref.shape
    blocks = gate_ref.shape[0]
    block_width = width // blocks
    taps = taps_ref.shape[0]

    @pl.when(pl.program_id(0) == 0)
    def _():
        padded[0:8, :] = edge_ref[...]
        carry[0] = jnp.ones((8, width), F32)
        carry[1] = jnp.zeros((8, width), F32)

    padded[8 : 8 + rows, :] = branch_ref[...]
    conv = jnp.broadcast_to(table_ref[0:1, :], (rows, width))
    for tap in range(taps):
        conv = conv + taps_ref[tap : tap + 1, :] * padded[8 - tap : 8 - tap + rows, :]
    padded[0:8, :] = branch_ref[rows - 8 : rows, :]
    conv_ref[...] = conv
    for block in range(blocks):
        columns = slice(block * block_width, (block + 1) * block_width)
        both = three_pass(conv[:, columns], gate_ref[block], ((1,), (0,)))
        a_rate = jax.nn.sigmoid(both[:, :block_width] + table_ref[1:2, columns])
        i_rate = jax.nn.sigmoid(both[:, block_width:] + table_ref[2:3, columns])
        decay, scale_in = decay_parts(a_rate, table_ref[3:4, columns])
        decay, value = tile_scan(decay, scale_in * i_rate * conv[:, columns], False)
        a_ref[:, columns] = a_rate
        i_ref[:, columns] = i_rate
        cumul_ref[:, columns] = decay
        state_ref[:, columns] = value
    carry[0], carry[1] = chain_tiles(cumul_ref, state_ref, carry[0], carry[1], False)
    pair_ref[...] = carry[...]


def backward_kernel(pre_ref, state_ref, a_ref, table_ref, *refs, chunks):
    mixed_refs = refs[:chunks]
    gate_grad_ref, suffix_ref, adjoint_ref, pair_ref, padded, carry = refs[chunks:]
    rows, width = pre_ref.shape
    chunk = (pl.num_programs(0) - 1 - pl.program_id(0)) * chunks // pl.num_programs(0)

    @pl.when(pl.program_id(0) == 0)
    def _():
        padded[rows : rows + 8, :] = jnp.ones((8, width), F32)
        carry[0] = jnp.ones((8, width), F32)
        carry[1] = jnp.zeros((8, width), F32)

    act, slope = gelu_parts(pre_ref[...])
    grad_mixed = mixed_refs[0][...]
    for place in range(1, chunks):
        grad_mixed = jnp.where(chunk == place, mixed_refs[place][...], grad_mixed)
    gate_grad_ref[...] = grad_mixed * state_ref[...] * slope
    decay = jnp.exp(-DECAY_CONST * a_ref[...] * table_ref[3:4, :])
    padded[0:rows, :] = decay
    shifted = padded[1 : rows + 1, :]
    padded[rows : rows + 8, :] = decay[0:8, :]
    shifted, value = tile_scan(shifted, grad_mixed * act, True)
    suffix_ref[...] = shifted
    adjoint_ref[...] = value
    carry[0], carry[1] = chain_tiles(suffix_ref, adjoint_ref, carry[0], carry[1], True)
    pair_ref[...] = carry[...] * decay[0:1, :][None]


def gradient_kernel(
    suffix_ref, adjoint_ref, conv_ref, a_ref, i_ref, state_ref, before_ref, branch_ref,
    incoming_ref, entry_ref, taps_ref, table_ref, gate_ref,
    branch_grad_ref, head_ref, sums_ref, gate_grad_ref,
    padded, shifted,
):
    rows, width = conv_ref.shape
    blocks = gate_ref.shape[0]
    block_width = width // blocks
    taps = taps_ref.shape[0]
    step, steps = pl.program_id(0), pl.num_programs(0)

    @pl.when(step == 0)
    def _():
        padded[rows : rows + 8, :] = jnp.zeros((8, width), F32)
        sums_ref[...] = jnp.zeros_like(sums_ref)
        gate_grad_ref[...] = jnp.zeros_like(gate_grad_ref)

    shifted[8 : 8 + rows, :] = state_ref[...]
    shifted[0:8, :] = jnp.where(step == steps - 1, entry_ref[...], before_ref[...])

    def total(values):
        return jnp.sum(values, axis=0, keepdims=True)

    for block in range(blocks):
        columns = slice(block * block_width, (block + 1) * block_width)
        adjoint = adjoint_ref[:, columns] + suffix_ref[:, columns] * incoming_ref[0:1, columns]
        conv, a_rate, i_rate = conv_ref[:, columns], a_ref[:, columns], i_ref[:, columns]
        soft_lambda = table_ref[3:4, columns]
        decay, scale_in = decay_parts(a_rate, soft_lambda)
        before = shifted[7 : 7 + rows, columns]
        weighted = adjoint * i_rate
        grad_log = adjoint * before * decay - weighted * conv * (decay * decay) / scale_in
        rate_part = grad_log * (-DECAY_CONST * a_rate)
        grad_a = rate_part * soft_lambda * (1.0 - a_rate)
        grad_i = weighted * scale_in * conv * (1.0 - i_rate)
        sums_ref[0:1, columns] += total(rate_part)
        sums_ref[1:2, columns] += total(grad_a)
        sums_ref[2:3, columns] += total(grad_i)
        both = jnp.concatenate([grad_a, grad_i], axis=1)
        gate_grad_ref[block] += three_pass(conv, both, ((0,), (0,)))
        back = three_pass(both, gate_ref[block], ((1,), (1,)))
        padded[0:rows, columns] = weighted * scale_in + back
    grad_conv = padded[0:rows, :]
    sums_ref[3:4, :] += total(grad_conv)
    head_ref[...] = grad_conv[0:8, :]
    branch = branch_ref[...]
    branch_grad = jnp.zeros((rows, width), F32)
    for tap in range(taps):
        moved = padded[tap : tap + rows, :]
        branch_grad = branch_grad + taps_ref[tap : tap + 1, :] * moved
        sums_ref[4 + tap : 5 + tap, :] += total(moved * branch)
    branch_grad_ref[...] = branch_grad
    padded[rows : rows + 8, :] = grad_conv[0:8, :]


def block_rows(rows):
    return 256 if rows % 1024 == 0 else rows // 4 if rows % 32 == 0 else rows


def fixed(*shape):
    return pl.BlockSpec(shape, lambda i: (0,) * len(shape))


def shaped(*shape):
    return jax.ShapeDtypeStruct(shape, F32)


def run_forward(branch, edges, taps, table, gates):
    rows, width = branch.shape
    step = block_rows(rows)
    moving = pl.BlockSpec((step, width), lambda i: (i, 0))
    return pl.pallas_call(
        forward_kernel,
        grid=(rows // step,),
        in_specs=[
            moving, fixed(8, width), fixed(*taps.shape), fixed(*table.shape), fixed(*gates.shape)
        ],
        out_specs=[moving] * 5 + [fixed(2, 8, width)],
        out_shape=[shaped(rows, width)] * 5 + [shaped(2, 8, width)],
        scratch_shapes=[pltpu.VMEM((step + 8, width), F32), pltpu.VMEM((2, 8, width), F32)],
        compiler_params=pltpu.CompilerParams(vmem_limit_bytes=VMEM_BYTES),
    )(branch, edges, taps, table, gates)


def run_backward(grad_mixed, gate_pre, rec_state, a_rate, table):
    rows, width = gate_pre.shape
    step = block_rows(rows)
    last, chunks = rows // step - 1, len(grad_mixed)
    each = rows // step // chunks
    moving = pl.BlockSpec((step, width), lambda i: (last - i, 0))

    def of_chunk(place):
        return pl.BlockSpec(
            (step, width), lambda i: (jnp.clip(last - i - place * each, 0, each - 1), 0)
        )

    return pl.pallas_call(
        functools.partial(backward_kernel, chunks=chunks),
        grid=(rows // step,),
        in_specs=[moving] * 3
        + [fixed(*table.shape)]
        + [of_chunk(place) for place in range(chunks)],
        out_specs=[moving] * 3 + [fixed(2, 8, width)],
        out_shape=[shaped(rows, width)] * 3 + [shaped(2, 8, width)],
        scratch_shapes=[pltpu.VMEM((step + 8, width), F32), pltpu.VMEM((2, 8, width), F32)],
        compiler_params=pltpu.CompilerParams(vmem_limit_bytes=VMEM_BYTES),
    )(gate_pre, rec_state, a_rate, table, *grad_mixed)


def run_gradient(
    suffix, adjoint, conv_out, a_rate, i_rate, rec_state, branch, incoming, entry, taps, table, gates
):
    rows, width = branch.shape
    step = block_rows(rows)
    last = rows // step - 1
    moving = pl.BlockSpec((step, width), lambda i: (last - i, 0))
    before = pl.BlockSpec(
        (8, width), lambda i: (jnp.maximum((last - i) * (step // 8) - 1, 0), 0)
    )
    return pl.pallas_call(
        gradient_kernel,
        grid=(rows // step,),
        in_specs=[moving] * 6
        + [before, moving, fixed(8, width), fixed(8, width)]
        + [fixed(*taps.shape), fixed(*table.shape), fixed(*gates.shape)],
        out_specs=[moving, fixed(8, width), fixed(8, width), fixed(*gates.shape)],
        out_shape=[
            shaped(rows, width), shaped(8, width), shaped(8, width), shaped(*gates.shape)
        ],
        scratch_shapes=[pltpu.VMEM((step + 8, width), F32), pltpu.VMEM((step + 8, width), F32)],
        compiler_params=pltpu.CompilerParams(vmem_limit_bytes=VMEM_BYTES),
    )(
        suffix, adjoint, conv_out, a_rate, i_rate, rec_state, rec_state, branch,
        incoming, entry, taps, table, gates,
    )


def product_kernel(span_ref, *refs, count, wide, split):
    left_refs, right_refs = refs[:count], refs[count : count + count * wide]
    outs, (high, low) = refs[count + count * wide : -2], refs[-2:]
    chunk, width = right_refs[0].shape

    @pl.when(pl.program_id(0) == 0)
    def _():
        for place, ref in enumerate(right_refs):
            row, column = place // wide * chunk, place % wide * width
            span = (slice(row, row + chunk), slice(column, column + width))
            high[span], low[span] = halves(ref[...])

    product = None
    for place, ref in enumerate(left_refs):
        span = slice(place * chunk, (place + 1) * chunk)
        left_high, left_low = halves(ref[...])

        def part(one, two):
            return lax.dot_general(
                one, two[span, :], (((0,), (0,)), ((), ())), preferred_element_type=F32
            )

        term = part(left_high, high) + (part(left_high, low) + part(left_low, high))
        product = term if product is None else product + term
    if not split:
        outs[0][...] = product
        return
    rows = product.shape[0] // 2
    first = span_ref[0] == 0
    zero, one = product[:rows], product[rows:]
    outs[0][0] = jnp.where(first, zero, one)
    outs[1][0] = jnp.where(first, one, zero)


def run_product(lefts, rights, wide, split):
    count = len(lefts)
    (chunk, depth), width = lefts[0].shape, rights[0].shape[1]
    shards = lax.axis_size("shard")
    rows = depth // (2 * shards)
    span = lax.axis_index("ctx").astype(jnp.int32).reshape(1)
    if split:
        out_specs = [pl.BlockSpec((1, rows, wide * width), lambda i, span: (i, 0, 0))] * 2
        out_shape = [shaped(shards, rows, wide * width)] * 2
    else:
        out_specs = [pl.BlockSpec((2 * rows, wide * width), lambda i, span: (i, 0))]
        out_shape = [shaped(depth, wide * width)]
    return pl.pallas_call(
        functools.partial(product_kernel, count=count, wide=wide, split=split),
        grid_spec=pltpu.PrefetchScalarGridSpec(
            num_scalar_prefetch=1,
            grid=(shards,),
            in_specs=[pl.BlockSpec((chunk, 2 * rows), lambda i, span: (0, i))] * count
            + [
                pl.BlockSpec(
                    (chunk, width), lambda i, span: (0, 0), pipeline_mode=pl.Buffered(1)
                )
            ]
            * (count * wide),
            out_specs=out_specs,
            scratch_shapes=[pltpu.VMEM((count * chunk, wide * width), BF16)] * 2,
        ),
        out_shape=out_shape,
        compiler_params=pltpu.CompilerParams(vmem_limit_bytes=VMEM_BYTES),
    )(span, *lefts, *rights)


def dot_parts(left_high, left_low, right_high, right_low, dims):
    def part(one, two):
        return lax.dot_general(one, two, (dims, ((), ())), preferred_element_type=F32)

    return part(left_high, right_high) + (part(left_high, right_low) + part(left_low, right_high))


def across_kernel(side_ref, *refs, count):
    lefts, rights = refs[:count], refs[count : 2 * count]
    kept_ref, sent_ref = refs[2 * count : 2 * count + 2]
    scratch = refs[2 * count + 2 :]

    @pl.when(pl.program_id(0) == 0)
    def _():
        for place, ref in enumerate(lefts):
            scratch[2 * place][...], scratch[2 * place + 1][...] = halves(ref[...])

    product = None
    for place in range(count):
        term = dot_parts(
            scratch[2 * place][...], scratch[2 * place + 1][...],
            *halves(rights[place][...]), ((1,), (1,)),
        )
        product = term if product is None else product + term
    half = kept_ref.shape[0]
    first = side_ref[0] == 0
    low, high = product[:half], product[half:]
    kept_ref[...] = jnp.where(first, low, high)
    sent_ref[...] = jnp.where(first, high, low)


def run_across(lefts, rights, chunk, rows):
    count, depth = len(lefts), rights[0].shape[0]
    step = 512 if depth % 512 == 0 else depth
    side = (lax.axis_index("tp") % 2).astype(jnp.int32).reshape(1)
    half = pl.BlockSpec((rows // 2, step), lambda i, side: (0, i))
    widths = [left.shape[1] for left in lefts]
    return pl.pallas_call(
        functools.partial(across_kernel, count=count),
        grid_spec=pltpu.PrefetchScalarGridSpec(
            num_scalar_prefetch=1,
            grid=(depth // step,),
            in_specs=[pl.BlockSpec((rows, w), lambda i, side: (chunk, 0)) for w in widths]
            + [pl.BlockSpec((step, w), lambda i, side: (i, 0)) for w in widths],
            out_specs=[half, half],
            scratch_shapes=[pltpu.VMEM((rows, w), BF16) for w in widths for _ in range(2)],
        ),
        out_shape=[shaped(rows // 2, depth)] * 2,
        compiler_params=pltpu.CompilerParams(vmem_limit_bytes=VMEM_BYTES),
    )(side, *lefts, *rights)


def up_product(value, pre):
    act, slope = gelu_parts(pre)
    return act * value, act, slope * value


def hidden_product(grad_hidden, act, slope_up):
    return grad_hidden * slope_up, grad_hidden * act


def norm_parts(rows):
    inv = lax.rsqrt(jnp.mean(rows * rows, axis=1, keepdims=True) + EPSILON)
    return inv, rows * inv


def norm_back(grad_normed, normed_hat, inv_scale, gain):
    grad_hat = grad_normed * gain
    inner = jnp.mean(grad_hat * normed_hat, axis=1, keepdims=True)
    return (inv_scale * (grad_hat - normed_hat * inner), jnp.sum(grad_normed * normed_hat, axis=0))


def on_device(
    inputs,
    lengths,
    rec_proj,
    gate_proj,
    out_proj,
    ffn_gate,
    ffn_up,
    ffn_down,
    conv_weight,
    conv_bias,
    a_gate,
    i_gate,
    a_bias,
    i_bias,
    lambda_param,
    rec_norm,
    ffn_norm,
    cotangent,
):
    seqs_here, span_len, width_model = inputs.shape
    row_count = seqs_here * span_len
    taps = conv_weight.shape[0]
    width_rec, width_ffn = rec_proj.shape[1], ffn_gate.shape[1]
    chunks = 4
    chunk_rows = row_count // chunks

    def rows_of(values, chunk):
        return values[chunk * chunk_rows : (chunk + 1) * chunk_rows]

    position = lax.axis_index("ctx") * span_len + jnp.arange(span_len, dtype=jnp.int32)
    valid_mask = position[None, :] < lengths[:, None]
    mask_rows = valid_mask.reshape(row_count, 1).astype(F32)

    two_level = lax.axis_size("ctx") == 2
    order = Sequence()
    chunk_list = list(range(chunks))
    scattered = []

    def weight_grad(lefts, rights, wide=1, split=True):
        count = len(lefts)
        if not two_level:
            total = order.step(
                lambda *a: matmul_tn(
                    jnp.concatenate(a[:count]),
                    jnp.concatenate(a[count:], axis=1 if wide > 1 else 0),
                ),
                *lefts, *rights,
            )
            return Box(scatter_plain(total.v))
        out = order.step(
            lambda *a: run_product(a[:count], a[count:], wide, split), *lefts, *rights
        )
        if split:
            return Scatter(*out, order, scattered)
        if scattered:
            order.wait(scattered[-1])
        scattered.append(Box(scatter_plain(order.gate(out[0])[0])))
        return scattered[-1]

    def start_ctx(grad):
        if isinstance(grad, Scatter):
            grad.start_ctx()

    def end_ctx(grad):
        if isinstance(grad, Scatter):
            grad.end_ctx()
            return grad.result
        return grad

    flat_in = inputs.reshape(row_count, width_model)
    flat_cot = cotangent.reshape(row_count, width_model)
    soft_lambda = jax.nn.softplus(-lambda_param)
    table = jnp.concatenate(
        [jnp.stack([conv_bias, a_bias, i_bias, soft_lambda]), jnp.zeros((4, width_rec), F32)]
    )
    gates = jnp.concatenate([a_gate, i_gate], axis=2)

    def norm_all(rows, gain):
        inv, hat = norm_parts(rows)
        return inv, hat * gain

    blocks = (rec_proj, gate_proj, out_proj, ffn_gate, ffn_up, ffn_down)
    turns = lax.axis_size("shard") - 1
    direct = two_level and turns == 3 and chunks == 4

    def partial_sum(lefts, weights, c):
        kept, sent = order.step(
            lambda *a: run_across(a[: len(lefts)], a[len(lefts) :], c, chunk_rows),
            *lefts, *weights,
        )
        return TpSum(kept, sent, order)

    def gathered(block, *earlier):
        order.wait(*earlier)
        return Box(gather_plain(order.gate(block)[0]))

    fg_weight = Box(gather_plain(ffn_gate))
    pending = []

    def tick(*sends):
        order.wait(*pending)
        pending[:] = [send() for send in sends]

    if direct:
        rec, gbr, out = (Gather(block, order) for block in blocks[:3])
        first = [gbr.swap(), out.swap(), rec.swap()]
        for _ in range(turns):
            tick(rec.turn)
        tick()
        order.wait(first[0], first[1])
        tick(gbr.turn_pair, *([rec.swap] * turns))
        late = pending[1:]
        del pending[1:]
        inv_one, normed_one = order.step(norm_all, flat_in, rec_norm)
        tick(gbr.turn_pair)
        order.wait(*late)
        rec_weight = rec.whole()
    else:
        rec_weight, gbr_weight, out_weight = (Box(gather_plain(block)) for block in blocks[:3])
        inv_one, normed_one = order.step(norm_all, flat_in, rec_norm)
    branch = order.step(matmul, normed_one, rec_weight)
    branch_end = order.step(lambda branch: branch[row_count - (taps - 1) :], branch)
    left_edges = order.send(passed_along, branch_end, "ctx", 1)
    if direct:
        tick(gbr.turn_pair)
        tick(out.turn_pair)
        gbr_weight = gbr.whole()
    gate_pre = order.step(matmul, normed_one, gbr_weight)
    if direct:
        tick(out.turn_pair)
    conv_out, a_rate, i_rate, cumul, local_state, pair = order.step(
        lambda branch, edges, *rest: run_forward(
            branch, jnp.pad(edges, ((8 - (taps - 1), 0), (0, 0))), *rest
        ),
        branch, left_edges, conv_weight, table, gates,
    )
    entry = Box(carried_in(pair.v[0], pair.v[1], 1))
    if direct:
        tick(out.turn_pair)
    fu_weight = gathered(ffn_up, fg_weight)

    def mix(local_state, cumul, entry, gate_pre):
        rec_state = local_state + cumul * entry[0:1]
        return rec_state, rec_state * gelu(gate_pre)

    rec_state, mixed_rows = order.step(mix, local_state, cumul, entry, gate_pre)
    if direct:
        tick()
        out_weight = out.whole()
    mix_sums, after_mix, inv_two, normed_two, gate_in, hidden, acts = (
        [None] * chunks for _ in range(7)
    )

    def start_mix(c):
        mix_sums[c] = partial_sum([mixed_rows], [out_weight], c)

    def take_mix(c):
        def norm_chunk(rows, kept, arriving, gain):
            rows = rows_of(rows, c) + mix_sums[c].rows(kept, arriving)
            inv, hat = norm_parts(rows)
            return rows, inv, hat * gain

        after_mix[c], inv_two[c], normed_two[c] = order.step(
            norm_chunk, flat_in, mix_sums[c].kept, mix_sums[c].arriving, ffn_norm
        )

    def run_gate(c):
        gate_in[c] = order.step(matmul, normed_two[c], fg_weight)

    def run_up(c):
        hidden[c], *acts[c] = order.step(
            lambda left, weight, pre: up_product(matmul(left, weight), pre),
            normed_two[c], fu_weight, gate_in[c],
        )

    grad_result = [None] * chunks

    def mask_chunk(c):
        grad_result[c] = order.step(
            lambda rows, mask: rows_of(rows, c) * rows_of(mask, c), flat_cot, mask_rows
        )

    start_mix(0)
    start_mix(1)
    mix_sums[0].cross()
    start_mix(2)
    mix_sums[1].cross()
    start_mix(3)
    for c in chunk_list:
        mask_chunk(c)
    mix_sums[0].share()
    mix_sums[2].cross()
    take_mix(0)
    run_gate(0)
    mix_sums[1].share()
    mix_sums[3].cross()
    take_mix(1)
    run_gate(1)
    fd_weight = gathered(ffn_down, fu_weight)
    run_up(0)
    mix_sums[2].share()
    run_up(1)
    take_mix(2)
    run_gate(2)
    run_up(2)
    mix_sums[3].share()
    take_mix(3)
    run_gate(3)
    run_up(3)

    ffn_sums, back_sums, grad_pre, grad_up = ([None] * chunks for _ in range(4))
    grad_after_mix, norm_two_sums, grad_mixed = ([None] * chunks for _ in range(3))
    block_out = None

    def start_ffn(c):
        ffn_sums[c] = partial_sum([hidden[c]], [fd_weight], 0)

    def take_ffn(c):
        nonlocal block_out

        def place(rows, kept, arriving, mask, block_out=None):
            rows = (rows + ffn_sums[c].rows(kept, arriving)) * rows_of(mask, c)
            if block_out is None:
                block_out = jnp.zeros((row_count, width_model), F32)
            return lax.dynamic_update_slice(block_out, rows, (c * chunk_rows, 0))

        block_out = order.step(
            place, after_mix[c], ffn_sums[c].kept, ffn_sums[c].arriving, mask_rows,
            *([block_out] if block_out else []),
        )

    def run_hidden(c):
        grad_pre[c], grad_up[c] = order.step(
            lambda left, weight, *acts: hidden_product(matmul(left, weight), *acts),
            grad_result[c], fd_weight, *acts[c],
        )

    def start_back(c):
        back_sums[c] = partial_sum([grad_pre[c], grad_up[c]], [fg_weight, fu_weight], 0)

    def take_back(c):
        def back(rows, after, inv, kept, arriving, gain):
            from_two, norm_sum = norm_back(
                back_sums[c].rows(kept, arriving), after * inv, inv, gain
            )
            return rows + from_two, norm_sum

        grad_after_mix[c], norm_two_sums[c] = order.step(
            back, grad_result[c], after_mix[c], inv_two[c],
            back_sums[c].kept, back_sums[c].arriving, ffn_norm,
        )
        grad_mixed[c] = order.step(matmul, grad_after_mix[c], out_weight)

    start_ffn(0)
    start_ffn(1)
    ffn_sums[0].cross()
    ffn_sums[1].cross()
    grad_fd = weight_grad(grad_result, hidden, split=False)
    run_hidden(3)
    start_back(3)
    ffn_sums[0].share()
    run_hidden(2)
    back_sums[3].cross()
    take_ffn(0)
    start_back(2)
    ffn_sums[1].share()
    run_hidden(1)
    back_sums[2].cross()
    take_ffn(1)
    start_back(1)
    back_sums[3].share()
    run_hidden(0)
    back_sums[1].cross()
    take_back(3)
    start_back(0)
    back_sums[2].share()
    grad_fg = weight_grad(normed_two, grad_pre, split=False)
    back_sums[0].cross()
    take_back(2)
    start_ffn(2)
    back_sums[1].share()
    start_ffn(3)
    ffn_sums[2].cross()
    take_back(1)
    grad_fu = weight_grad(normed_two, grad_up)
    start_ctx(grad_fu)
    back_sums[0].share()
    ffn_sums[3].cross()
    take_back(0)

    grad_gate_pre, suffix, local_adjoint, back_pair = order.step(
        lambda pre, state, rate, table, *mixed: run_backward(mixed, pre, state, rate, table),
        gate_pre, rec_state, a_rate, table, *grad_mixed,
    )
    incoming = Box(carried_in(back_pair.v[0], back_pair.v[1], -1))
    grad_branch, head, sums, grad_gates = order.step(
        run_gradient,
        suffix, local_adjoint, conv_out, a_rate, i_rate, rec_state, branch, incoming, entry,
        conv_weight, table, gates,
    )
    head = order.step(lambda head: head[: taps - 1], head)
    right_edges = order.send(passed_along, head, "ctx", -1)

    def tail_rows(grad_branch, right_edges, conv_weight):
        tail = grad_branch[row_count - (taps - 1) :]
        padded_edges = jnp.concatenate([jnp.zeros_like(right_edges), right_edges])
        for tap in range(1, taps):
            tail = tail + conv_weight[tap] * padded_edges[tap : tap + taps - 1]
        return lax.dynamic_update_slice(grad_branch, tail, (row_count - (taps - 1), 0))

    one_sums = [None] * chunks

    def start_one(c):
        one_sums[c] = partial_sum([grad_branch, grad_gate_pre], [rec_weight, gbr_weight], c)

    input_grad = None

    def take_one(c):
        nonlocal input_grad

        def back(rows, after, inv, kept, arriving, gain, grads=None):
            inv = rows_of(inv, c)
            from_one, _ = norm_back(
                one_sums[c].rows(kept, arriving), rows_of(after, c) * inv, inv, gain
            )
            if grads is None:
                grads = jnp.zeros((row_count, width_model), F32)
            return lax.dynamic_update_slice(grads, rows + from_one, (c * chunk_rows, 0))

        input_grad = order.step(
            back, grad_after_mix[c], flat_in, inv_one,
            one_sums[c].kept, one_sums[c].arriving, rec_norm,
            *([input_grad] if input_grad else []),
        )

    def small_parts(sums, head, left_edges, grad_gates, lambda_param, *norm_two):
        padded_head = jnp.concatenate([left_edges, jnp.zeros_like(left_edges)])
        edge = taps - 1
        grad_taps = [sums[4]] + [
            sums[4 + tap] + jnp.sum(head * padded_head[edge - tap : 2 * edge - tap], axis=0)
            for tap in range(1, taps)
        ]
        grad_lambda = sums[0] * -jax.nn.sigmoid(-lambda_param)
        vectors = jnp.stack([*grad_taps, sums[1], sums[2], sums[3], grad_lambda])
        return jnp.concatenate(
            [grad_gates.reshape(-1, 128), vectors.reshape(-1, 128), sum(norm_two).reshape(-1, 128)]
        )

    start_one(0)
    ffn_sums[2].share()
    start_one(1)
    one_sums[0].cross()
    grad_fu = end_ctx(grad_fu)
    take_ffn(2)
    grad_branch = order.step(tail_rows, grad_branch, right_edges, conv_weight)
    grad_recs = weight_grad([normed_one], [grad_branch, grad_gate_pre], wide=2)
    rec_parts = grad_recs
    start_ctx(grad_recs)
    ffn_sums[3].share()
    start_one(2)
    one_sums[1].cross()
    take_ffn(3)
    small = order.step(
        small_parts, sums, head, left_edges, grad_gates, lambda_param, *norm_two_sums
    )
    small = SmallSum(small, order, ("ctx", "shard"))
    small.advance()
    start_one(3)
    one_sums[0].share()
    grad_out_proj = weight_grad(
        grad_after_mix, order.step(lambda rows: [rows_of(rows, c) for c in chunk_list], mixed_rows)
    )
    one_sums[2].cross()
    take_one(0)
    small.advance()
    block_out = block_out.v.reshape(seqs_here, span_len, width_model)

    if two_level:
        span = lax.axis_index("ctx")

        def gain_sums(kept, sent, gain, rec_weight, gbr_weight):
            def rows_sum(grads, which):
                total = 0.0
                for place, weight in enumerate((rec_weight, gbr_weight)):
                    split = weight.reshape(turns + 1, 2, -1, width_rec)
                    split = lax.dynamic_index_in_dim(split, which, 1, keepdims=False)
                    grad = grads[:, :, place * width_rec : (place + 1) * width_rec]
                    total = total + jnp.sum(grad * split, axis=2)
                return total

            kept, sent = rows_sum(kept, span), rows_sum(sent, 1 - span)
            both = jnp.stack(
                [jnp.where(span == 0, kept, sent), jnp.where(span == 0, sent, kept)], axis=1
            )
            return (both.reshape(-1) / gain).reshape(-1, 128)

        norm_one_sum = order.step(
            gain_sums, rec_parts.kept, rec_parts.sent, rec_norm, rec_weight, gbr_weight
        )
    else:
        def gain_sums(grads, more, normed, gain, first, second):
            back = matmul_nt(grads, first) + matmul_nt(more, second)
            return (jnp.sum(back * normed, axis=0) / gain).reshape(-1, 128)

        norm_one_sum = order.step(
            gain_sums, grad_branch, grad_gate_pre, normed_one, rec_norm, rec_weight, gbr_weight
        )
    tiny = SmallSum(norm_one_sum, order, ("tp", "ctx", "shard"))
    one_sums[1].share()
    tiny.advance()
    one_sums[3].cross()
    take_one(1)
    tiny.advance()
    grad_recs = end_ctx(grad_recs)
    start_ctx(grad_out_proj)
    small.advance()
    one_sums[2].share()
    tiny.advance()
    take_one(2)
    tiny.advance()
    small.advance()
    grad_out_proj = end_ctx(grad_out_proj)
    tiny.advance()
    one_sums[3].share()
    tiny.advance()
    take_one(3)
    for left in (small, tiny):
        while left.advance():
            pass
    input_grad = input_grad.v.reshape(seqs_here, span_len, width_model)
    small = small.value.v
    sum_norm_one = tiny.value.v.reshape(-1)
    gate_rows = gates.size // 128
    vector_rows = (taps + 4) * width_rec // 128
    sum_gates = small[:gate_rows].reshape(gates.shape)
    vectors = small[gate_rows : gate_rows + vector_rows].reshape(taps + 4, width_rec)
    sum_norm_two = small[gate_rows + vector_rows :].reshape(-1)
    sum_conv_weight = vectors[:taps]
    sum_a_bias, sum_i_bias, sum_conv_bias, sum_lambda = (vectors[taps + k] for k in range(4))
    grad_recs, grad_out_proj, grad_fg, grad_fu, grad_fd = (
        grad.v for grad in (grad_recs, grad_out_proj, grad_fg, grad_fu, grad_fd)
    )
    grad_rec_proj, grad_gate_proj = grad_recs[:, :width_rec], grad_recs[:, width_rec:]
    block_width = a_gate.shape[2]
    return (
        block_out,
        input_grad,
        grad_rec_proj,
        grad_gate_proj,
        grad_out_proj,
        grad_fg,
        grad_fu,
        grad_fd,
        sum_conv_weight,
        sum_conv_bias,
        sum_gates[:, :, :block_width],
        sum_gates[:, :, block_width:],
        sum_a_bias,
        sum_i_bias,
        sum_lambda,
        sum_norm_one,
        sum_norm_two,
    )


def solution(mesh):
    placed = (
        P("shard", "ctx", None),
        P("shard"),
        P(("shard", "ctx"), "tp"),
        P(("shard", "ctx"), "tp"),
        P(("shard", "ctx"), "tp"),
        P(("shard", "ctx"), "tp"),
        P(("shard", "ctx"), "tp"),
        P(("shard", "ctx"), "tp"),
        P(None, "tp"),
        P("tp"),
        P("tp", None, None),
        P("tp", None, None),
        P("tp"),
        P("tp"),
        P("tp"),
        P(),
        P(),
        P("shard", "ctx", None),
    )
    return jax.shard_map(
        on_device,
        mesh=mesh,
        in_specs=placed,
        out_specs=(
            P("shard", "ctx", None),
            P("shard", "ctx", None),
            P(("shard", "ctx"), "tp"),
            P(("shard", "ctx"), "tp"),
            P(("shard", "ctx"), "tp"),
            P(("shard", "ctx"), "tp"),
            P(("shard", "ctx"), "tp"),
            P(("shard", "ctx"), "tp"),
            P(None, "tp"),
            P("tp"),
            P("tp", None, None),
            P("tp", None, None),
            P("tp"),
            P("tp"),
            P("tp"),
            P(),
            P(),
        ),
        check_vma=False,
    )
```

time: 3150 us -> 1310 us (0.42)
  waiting for transfers between devices: 1420 us -> 394 us
  matrix products: 818 us -> 166 us
  local copies, waits for them, and re-layouts: 589 us -> 84.5 us
  Pallas kernels: 0 us -> 382 us
  starting transfers between devices: 6.91 us -> 80 us
  other arithmetic: 230 us -> 174 us
  blocking collectives: 55.2 us -> 0 us
    dot_general x24 -> x18, matrix products: 818 us -> 166 us  [matmul(): return jnp.dot(left, right, precision=HIGH, preferred_element_type=F32)]
    reduce_scatter x6 -> x5, waiting for transfers between devices: 629 us -> 14.8 us  [the longest x3 14.7 us: over_shard(): lax.psum_scatter(rows.reshape(shards * count, width), 'shard', scatter_di...]
    psum x4 -> x0, waiting for transfers between devices: 499 us -> none  [the longest x1 217 us: on_device(): mix_total = lax.psum(matmul_nt(mixed_rows, out_weight), 'tp')]
    pallas_call x0 -> x24, Pallas kernels: none -> 382 us  [the longest x16 179 us: run_across(): pl.pallas_call(functools.partial(across_kernel, count=count), grid_spec=p...]
    ppermute x0 -> x74, waiting for transfers between devices: none -> 312 us  [the longest x65 227 us: swapped(): lax.ppermute(block, axis, [(i, i ^ bit) for i in range(lax.axis_size(axis...]
    slice x161 -> x28, local copies, waits for them, and re-layouts: 302 us -> 10.5 us  [the longest x17 4.3 us: rows_of(): return values[chunk * chunk_rows:(chunk + 1) * chunk_rows]]
    all_gather x6 -> x3, waiting for transfers between devices: 285 us -> 18 us  [gather_plain(): return lax.all_gather(block, ('shard', 'ctx'), axis=0, tiled=True)]
    pad x80 -> x1, local copies, waits for them, and re-layouts: 164 us -> 0.61 us  [on_device(): jnp.pad(edges, ((8 - (taps - 1), 0), (0, 0)))]
  transfers between devices with their start and end apart: 18 -> 86, of which waited for: 14 -> 28; matrix products, arithmetic and copies ran while one was open for 30% -> 29% of each run, Pallas kernels for 0% -> 26%
where the time goes in v1:
time: 1310 us; the launch traced here: 1300 us
  waiting for transfers between devices  394 us (30%)
  Pallas kernels  382 us (29%)
  other arithmetic  174 us (13%)
  matrix products  166 us (13%)
  local copies, waits for them, and re-layouts  84.5 us (6%)
  starting transfers between devices  80 us (6%)
  between operations  16.9 us (1%)
    ppermute x65, waiting for transfers between devices, swapped(): lax.ppermute(block, axis, [(i, i ^ bit) for i in range(lax.axis_size(axis...  227 us
    pallas_call x16, Pallas kernels, run_across(): pl.pallas_call(functools.partial(across_kernel, count=count), grid_spec=p...  179 us
    dot_general x18, matrix products, matmul(): return jnp.dot(left, right, precision=HIGH, preferred_element_type=F32)  166 us
    pallas_call x5, Pallas kernels, run_product(): pl.pallas_call(functools.partial(product_kernel, count=count, wide=wide,...  142 us
    ppermute x9, waiting for transfers between devices, rotated(): lax.ppermute(block, axis, [(i, (i + distance) % count) for i in range(cou...  85.7 us
    ppermute x65, starting transfers between devices, swapped(): lax.ppermute(block, axis, [(i, i ^ bit) for i in range(lax.axis_size(axis...  48.3 us
    ppermute x4, waiting for transfers between devices, passed_along(): return lax.ppermute(block, axis, route)  47.9 us
    unnamed x209, local copies, waits for them, and re-layouts  37.8 us
  transfers between devices with their start and end apart: 86, of which 28 were waited for; matrix products, arithmetic and copies ran while one was open for 29% of the time, Pallas kernels for 26%

profile of v1, /device:TPU:0, one launch (start us, length us, event | category | flops | bytes accessed | tf_op | source)
XLA Modules:
  0.0 1297.3 jit_solution(436340396561997610)
XLA Ops:
  23.0 21.4 %collective-permute-done.1 = f32[192,512]{1,0:T(8,128)} collective-permute-done((f32[192,512]{1,0:T(8,128)}, f32[192,512]{1,0:T(8,128)}, u32[]{:S(2)}, u32[]{:S(2)}) %collective-permute-start.1) | collective-permute-done | bytes 393248 | tf_op jit(solution)/shard_map/ppermute | solution.py:85
  52.2 18.1 %collective-permute-done.2 = f32[192,512]{1,0:T(8,128)S(1)} collective-permute-done((f32[192,512]{1,0:T(8,128)}, f32[192,512]{1,0:T(8,128)S(1)}, u32[]{:S(2)}, u32[]{:S(2)}) %collective-permute-start.2) | collective-permute-done | bytes 393248 | tf_op jit(solution)/shard_map/ppermute | solution.py:85
  81.4 10.5 multiply_multiply_fusion.refs_0_
  92.9 25.2 %collective-permute-done.6 = f32[192,512]{1,0:T(8,128)} collective-permute-done((f32[192,512]{1,0:T(8,128)}, f32[192,512]{1,0:T(8,128)}, u32[]{:S(2)}, u32[]{:S(2)}) %collective-permute-start.6) | collective-permute-done | bytes 393248 | tf_op jit(solution)/shard_map/ppermute | solution.py:89
  122.1 14.5 %fusion.41.branch_ref = f32[2048,512]{1,0:T(8,128)S(1)} fusion(f32[2048,1536]{1,0:T(8,128)} %multiply_multiply_fusion.refs_0_, f32[1536,512]{1,0:T(8,128)S(1)} %bitcast.211), kind=kOutput, calls=%fused_computation.210 | convolution fusion | flops 9663676416 | bytes 19922944 | tf_op jit(solution)/shard_map/dot_general | solution.py:21
  136.7 20.2 %collective-permute-done.10 = f32[2,192,512]{2,1,0:T(8,128)S(1)} collective-permute-done((f32[2,192,512]{2,1,0:T(8,128)}, f32[2,192,512]{2,1,0:T(8,128)S(1)}, u32[]{:S(2)}, u32[]{:S(2)}) %collective-permute-start.10) | collective-permute-done | bytes 786464 | tf_op jit(solution)/shard_map/ppermute | solution.py:85
  156.8 8.7 collective-permute-start.11
  171.9 9.7 collective-permute-done.11
  183.5 11.5 fusion.42.pre_ref
  201.8 18.1 %shard_map.305 = (f32[2048,512]{1,0:T(8,128)}, f32[2048,512]{1,0:T(8,128)}, f32[2048,512]{1,0:T(8,128)}, f32[2048,512]{1,0:T(8,128)}, f32[2048,512]{1,0:T(8,128)}, /*index=5*/f32[2,8,512]{2,1,0:T(8,128)}) custom-call(f32[2048,512]{1,0:T(8,128)} %copy-done.40, f32[8,512]{1,0:T(8,128)} %pad.8.edge_ref, f32[4,512]{1,0:T(4,128)} %taps_ref.1, ...), custom_call_target="tpu_custom_call" | custom-call | tf_op jit(solution)/shard_map/pallas_call | solution.py:454
  317.4 17.0 %collective-permute-done.22 = f32[256,1536]{1,0:T(8,128)S(1)} collective-permute-done((f32[256,1536]{1,0:T(8,128)}, f32[256,1536]{1,0:T(8,128)S(1)}, u32[]{:S(2)}, u32[]{:S(2)}) %collective-permute-start.22) | collective-permute-done | bytes 1572896 | tf_op jit(solution)/shard_map/ppermute | solution.py:89
  345.6 8.6 fusion.44
  354.2 12.4 all-gather.6.cloned.1.call-done.refs_3_
  368.2 12.9 add_multiply_fusion.3
  381.1 21.6 %collective-permute-done.25 = f32[256,1536]{1,0:T(8,128)S(1)} collective-permute-done((f32[256,1536]{1,0:T(8,128)}, f32[256,1536]{1,0:T(8,128)S(1)}, u32[]{:S(2)}, u32[]{:S(2)}) %collective-permute-start.25) | collective-permute-done | bytes 1572896 | tf_op jit(solution)/shard_map/ppermute | solution.py:89
  404.5 12.5 add_multiply_fusion.2
  432.4 12.5 add_multiply_fusion.1
  459.8 10.5 add_multiply_fusion
  475.8 10.6 shard_map.310
  486.4 10.7 shard_map.311
  502.2 32.9 %shard_map.312 = f32[1536,1152]{1,0:T(8,128)} custom-call(s32[1]{0:T(128)} %bitcast.1.span_ref, f32[512,1536]{1,0:T(8,128)} %slice_multiply_fusion.7.refs_0_, f32[512,1536]{1,0:T(8,128)} %slice_multiply_fusion.6.refs_1_, f32[512,1536]{1,0:T(8,128)} %slice_multiply_fusion.5.refs_2_, f32[512,1536]{1,0:T(8,128)} %slice_multiply_fusion.4.refs_3_, ...), custom_call_target="tpu_custom_call" | custom-call | tf_op jit(solution)/shard_map/pallas_call | solution.py:566
  537.0 12.8 fusion.36
  549.9 18.5 %shard_map.313 = (f32[256,1536]{1,0:T(8,128)}, f32[256,1536]{1,0:T(8,128)}) custom-call(s32[1]{0:T(128)} %bitcast.side_ref, f32[512,1152]{1,0:T(8,128)} %get-tuple-element.896.refs_0_.refs_7_, f32[512,1152]{1,0:T(8,128)} %get-tuple-element.944.refs_1_.refs_7_, f32[1536,1152]{1,0:T(8,128)} %all-gather.4.cloned.1.call-done.refs_2_, ...), custom_call_target="tpu_custom_call" | custom-call | tf_op jit(solution)/shard_map/pallas_call | solution.py:623
  576.1 11.0 fusion.35
  597.2 18.5 %shard_map.314 = (f32[256,1536]{1,0:T(8,128)}, f32[256,1536]{1,0:T(8,128)}) custom-call(s32[1]{0:T(128)} %bitcast.side_ref, f32[512,1152]{1,0:T(8,128)} %get-tuple-element.895.refs_0_.refs_6_, f32[512,1152]{1,0:T(8,128)} %get-tuple-element.943.refs_1_.refs_6_, f32[1536,1152]{1,0:T(8,128)} %all-gather.4.cloned.1.call-done.refs_2_, ...), custom_call_target="tpu_custom_call" | custom-call | tf_op jit(solution)/shard_map/pallas_call | solution.py:623
  619.0 10.5 fusion.34
  634.9 18.6 %shard_map.315 = (f32[256,1536]{1,0:T(8,128)}, f32[256,1536]{1,0:T(8,128)}) custom-call(s32[1]{0:T(128)} %bitcast.side_ref, f32[512,1152]{1,0:T(8,128)} %get-tuple-element.894.refs_0_.refs_5_, f32[512,1152]{1,0:T(8,128)} %get-tuple-element.942.refs_1_.refs_5_, f32[1536,1152]{1,0:T(8,128)} %all-gather.4.cloned.1.call-done.refs_2_, ...), custom_call_target="tpu_custom_call" | custom-call | tf_op jit(solution)/shard_map/pallas_call | solution.py:623
  658.1 10.4 fusion.33
  679.9 18.5 %shard_map.316 = (f32[256,1536]{1,0:T(8,128)}, f32[256,1536]{1,0:T(8,128)}) custom-call(s32[1]{0:T(128)} %bitcast.side_ref, f32[512,1152]{1,0:T(8,128)} %get-tuple-element.893.refs_0_.refs_4_, f32[512,1152]{1,0:T(8,128)} %get-tuple-element.941.refs_1_.refs_4_, f32[1536,1152]{1,0:T(8,128)} %all-gather.4.cloned.1.call-done.refs_2_, ...), custom_call_target="tpu_custom_call" | custom-call | tf_op jit(solution)/shard_map/pallas_call | solution.py:623
  701.6 32.9 %shard_map.317 = f32[1536,1152]{1,0:T(8,128)} custom-call(s32[1]{0:T(128)} %bitcast.1.span_ref, f32[512,1536]{1,0:T(8,128)} %copy-done.23, f32[512,1536]{1,0:T(8,128)} %copy-done.24, f32[512,1536]{1,0:T(8,128)} %copy-done.28, f32[512,1536]{1,0:T(8,128)} %copy-done.29, f32[512,1152]{1,0:T(8,128)} %get-tuple-element.893.refs_0_.refs_4_, ...), custom_call_target="tpu_custom_call" | custom-call | tf_op jit(solution)/shard_map/pallas_call | solution.py:566
  750.2 10.6 shard_map.318
  761.0 11.4 collective-permute-done.43
  775.8 10.5 shard_map.319
  799.2 33.2 %shard_map.320 = (f32[4,192,1152]{2,1,0:T(8,128)}, f32[4,192,1152]{2,1,0:T(8,128)}) custom-call(s32[1]{0:T(128)} %bitcast.1.span_ref, f32[512,1536]{1,0:T(8,128)} %copy-done.23, f32[512,1536]{1,0:T(8,128)} %copy-done.24, f32[512,1536]{1,0:T(8,128)} %copy-done.28, f32[512,1536]{1,0:T(8,128)} %copy-done.29, f32[512,1152]{1,0:T(8,128)} %get-tuple-element.941.refs_1_.refs_4_, ...), custom_call_target="tpu_custom_call" | custom-call | tf_op jit(solution)/shard_map/pallas_call | solution.py:566
  848.3 18.8 %shard_map.321 = (f32[2048,512]{1,0:T(8,128)}, f32[2048,512]{1,0:T(8,128)}, f32[2048,512]{1,0:T(8,128)}, f32[2,8,512]{2,1,0:T(8,128)}) custom-call(f32[2048,512]{1,0:T(8,128)} %fusion.42.pre_ref, f32[2048,512]{1,0:T(8,128)} %get-tuple-element.987.state_ref.before_ref, f32[2048,512]{1,0:T(8,128)} %get-tuple-element.985.a_ref, ...), custom_call_target="tpu_custom_call" | custom-call | tf_op jit(solution)/shard_map/pallas_call | solution.py:479
  869.1 47.9 %collective-permute-done.49.incoming_ref = f32[8,512]{1,0:T(8,128)S(1)} collective-permute-done((f32[8,512]{1,0:T(8,128)S(1)}, f32[8,512]{1,0:T(8,128)S(1)}, u32[]{:S(2)}, u32[]{:S(2)}) %collective-permute-start.49) | collective-permute-done | bytes 16416 | tf_op jit(solution)/shard_map/ppermute | solution.py:80
  917.6 23.9 %shard_map.322 = (f32[2048,512]{1,0:T(8,128)}, f32[8,512]{1,0:T(8,128)}, f32[8,512]{1,0:T(8,128)}, f32[4,128,256]{2,1,0:T(8,128)}) custom-call(f32[2048,512]{1,0:T(8,128)} %get-tuple-element.982.suffix_ref, f32[2048,512]{1,0:T(8,128)} %get-tuple-element.983.adjoint_ref, f32[2048,512]{1,0:T(8,128)} %get-tuple-element.984.conv_ref, ...), custom_call_target="tpu_custom_call" | custom-call | tf_op jit(solution)/shard_map/pallas_call | solution.py:502
  942.2 9.1 shard_map.323
  954.8 9.5 shard_map.324
  976.4 27.2 %shard_map.325 = (f32[4,192,1024]{2,1,0:T(8,128)}, f32[4,192,1024]{2,1,0:T(8,128)}) custom-call(s32[1]{0:T(128)} %bitcast.1.span_ref, f32[2048,1536]{1,0:T(8,128)} %multiply_multiply_fusion.refs_0_, f32[2048,512]{1,0:T(8,128)} %dynamic_update_slice.127.refs_1_.refs_0_, f32[2048,512]{1,0:T(8,128)} %get-tuple-element.1070.refs_1_.refs_2_), custom_call_target="tpu_custom_call" | custom-call | tf_op jit(solution)/shard_map/pallas_call | solution.py:566
  1006.8 9.0 shard_map.326
  1023.6 9.2 shard_map.327
  1032.8 9.9 collective-permute-done.58
  1052.0 15.7 %shard_map.328 = (f32[4,192,512]{2,1,0:T(8,128)}, f32[4,192,512]{2,1,0:T(8,128)}) custom-call(s32[1]{0:T(128)} %bitcast.1.span_ref, f32[512,1536]{1,0:T(8,128)} %copy-done.30, f32[512,1536]{1,0:T(8,128)} %copy-done.26, f32[512,1536]{1,0:T(8,128)} %copy-done.21, f32[512,1536]{1,0:T(8,128)} %copy-done.19, f32[512,512]{1,0:T(8,128)} %get-tuple-element.1083.refs_4_, ...), custom_call_target="tpu_custom_call" | custom-call | tf_op jit(solution)/shard_map/pallas_call | solution.py:566
  1101.7 59.3 %collective-permute-done.68 = f32[4,192,1024]{2,1,0:T(8,128)} collective-permute-done((f32[4,192,1024]{2,1,0:T(8,128)S(1)}, f32[4,192,1024]{2,1,0:T(8,128)}, u32[]{:S(2)}, u32[]{:S(2)}) %collective-permute-start.68) | collective-permute-done | bytes 3145760 | tf_op jit(solution)/shard_map/ppermute | solution.py:89
  1169.8 31.0 %collective-permute-done.62 = f32[1068,128]{1,0:T(8,128)S(1)} collective-permute-done((f32[1068,128]{1,0:T(8,128)}, f32[1068,128]{1,0:T(8,128)S(1)}, u32[]{:S(2)}, u32[]{:S(2)}) %collective-permute-start.62) | collective-permute-done | bytes 546848 | tf_op jit(solution)/shard_map/ppermute | solution.py:89
  1220.8 31.0 %collective-permute-done.72 = f32[1068,128]{1,0:T(8,128)S(1)} collective-permute-done((f32[1068,128]{1,0:T(8,128)S(1)}, f32[1068,128]{1,0:T(8,128)S(1)}, u32[]{:S(2)}, u32[]{:S(2)}) %collective-permute-start.72) | collective-permute-done | bytes 546848 | tf_op jit(solution)/shard_map/ppermute | solution.py:89
  1275.4 14.7 %reduce-scatter.14.cloned.1.call-done = f32[192,512]{1,0:T(8,128)} async-done(((f32[768,512]{1,0:T(8,128)}), f32[192,512]{1,0:T(8,128)}) %reduce-scatter.14.cloned.1.call-update) | async-done | bytes 393232 | tf_op jit(solution)/shard_map/reduce_scatter | solution.py:189
  (582 shorter events, 426.7 us)
Async XLA Ops:
  7.2 221.2 %all-gather.4.cloned.1.call-start = ((), (), s32[]{:S(2)}) async-start(), calls=%async_computation.5 | async-start | bytes 7962624 | tf_op jit(solution)/shard_map/all_gather | solution.py:184
  8.0 358.7 %all-gather.6.cloned.1.call-start = ((), (), s32[]{:S(2)}) async-start(), calls=%async_computation.6 | async-start | bytes 7962624 | tf_op jit(solution)/shard_map/all_gather | solution.py:184
  11.1 40.0 %collective-permute-start.9 = (f32[192,512]{1,0:T(8,128)}, f32[192,512]{1,0:T(8,128)}, u32[]{:S(2)}, u32[]{:S(2)}) collective-permute-start(f32[192,512]{1,0:T(8,128)} %param.20), channel_id=1, source_target_pairs={{0,4},{4,0},{1,5},{5,1},{2,6},{6,2},{3,7},{7,3},{8,12},{12,8},{9,1... | collective-permute-start | bytes 1179656 | tf_op jit(solution)/shard_map/ppermute | solution.py:89
  12.6 39.6 %collective-permute-start.3 = (f32[192,512]{1,0:T(8,128)}, f32[192,512]{1,0:T(8,128)}, u32[]{:S(2)}, u32[]{:S(2)}) collective-permute-start(f32[192,512]{1,0:T(8,128)} %param.21), channel_id=1, source_target_pairs={{0,4},{4,0},{1,5},{5,1},{2,6},{6,2},{3,7},{7,3},{8,12},{12,8},{9,1... | collective-permute-start | bytes 1179656 | tf_op jit(solution)/shard_map/ppermute | solution.py:89
  13.1 39.1 %collective-permute-start.4 = (f32[192,512]{1,0:T(8,128)}, f32[192,512]{1,0:T(8,128)}, u32[]{:S(2)}, u32[]{:S(2)}) collective-permute-start(f32[192,512]{1,0:T(8,128)} %param.22), channel_id=1, source_target_pairs={{0,4},{4,0},{1,5},{5,1},{2,6},{6,2},{3,7},{7,3},{8,12},{12,8},{9,1... | collective-permute-start | bytes 1179656 | tf_op jit(solution)/shard_map/ppermute | solution.py:89
  71.5 48.9 %collective-permute-start.5 = (f32[2,192,512]{2,1,0:T(8,128)S(1)}, f32[2,192,512]{2,1,0:T(8,128)}, u32[]{:S(2)}, u32[]{:S(2)}) collective-permute-start(f32[2,192,512]{2,1,0:T(8,128)S(1)} %pad_maximum_fusion.4), channel_id=1, source_target_pairs={{0,8},{8,16},{16,24},{24,0},{1,9},{9,17},{17,25},{25,1},{2,10},{10... | collective-permute-start | bytes 2359304 | tf_op jit(solution)/shard_map/ppermute | solution.py:85
  71.6 48.7 %collective-permute-start.8 = (f32[192,512]{1,0:T(8,128)S(1)}, f32[192,512]{1,0:T(8,128)S(1)}, u32[]{:S(2)}, u32[]{:S(2)}) collective-permute-start(f32[192,512]{1,0:T(8,128)S(1)} %collective-permute-done.2), channel_id=1, source_target_pairs={{0,4},{4,0},{1,5},{5,1},{2,6},{6,2},{3,7},{7,3},{8,12},{12,8},{9,1... | collective-permute-start | bytes 1179656 | tf_op jit(solution)/shard_map/ppermute | solution.py:89
  73.2 47.0 %collective-permute-start.7 = (f32[192,512]{1,0:T(8,128)}, f32[192,512]{1,0:T(8,128)S(1)}, u32[]{:S(2)}, u32[]{:S(2)}) collective-permute-start(f32[192,512]{1,0:T(8,128)} %collective-permute-done.1), channel_id=1, source_target_pairs={{0,4},{4,0},{1,5},{5,1},{2,6},{6,2},{3,7},{7,3},{8,12},{12,8},{9,1... | collective-permute-start | bytes 1179656 | tf_op jit(solution)/shard_map/ppermute | solution.py:89
  73.7 44.5 %collective-permute-start.6 = (f32[192,512]{1,0:T(8,128)}, f32[192,512]{1,0:T(8,128)}, u32[]{:S(2)}, u32[]{:S(2)}) collective-permute-start(f32[192,512]{1,0:T(8,128)} %collective-permute-done), channel_id=1, source_target_pairs={{0,4},{4,0},{1,5},{5,1},{2,6},{6,2},{3,7},{7,3},{8,12},{12,8},{9,1... | collective-permute-start | bytes 1179656 | tf_op jit(solution)/shard_map/ppermute | solution.py:89
  120.4 36.4 %collective-permute-start.10 = (f32[2,192,512]{2,1,0:T(8,128)}, f32[2,192,512]{2,1,0:T(8,128)S(1)}, u32[]{:S(2)}, u32[]{:S(2)}) collective-permute-start(f32[2,192,512]{2,1,0:T(8,128)} %collective-permute-done.5), channel_id=1, source_target_pairs={{0,8},{8,16},{16,24},{24,0},{1,9},{9,17},{17,25},{25,1},{2,10},{10... | collective-permute-start | bytes 2359304 | tf_op jit(solution)/shard_map/ppermute | solution.py:85
  166.0 34.6 %collective-permute-start.13 = (f32[3,512]{1,0:T(4,128)S(1)}, f32[3,512]{1,0:T(4,128)S(1)}, u32[]{:S(2)}, u32[]{:S(2)}) collective-permute-start(f32[3,512]{1,0:T(4,128)S(1)} %slice.265), channel_id=1, source_target_pairs={{0,4},{1,5},{2,6},{3,7},{8,12},{9,13},{10,14},{11,15},{16,20},{17,... | collective-permute-start | bytes 18440 | tf_op jit(solution)/shard_map/ppermute | solution.py:80
  200.6 26.3 %collective-permute-start.14 = (f32[2,192,512]{2,1,0:T(8,128)S(1)}, f32[2,192,512]{2,1,0:T(8,128)}, u32[]{:S(2)}, u32[]{:S(2)}) collective-permute-start(f32[2,192,512]{2,1,0:T(8,128)S(1)} %collective-permute-done.12), channel_id=1, source_target_pairs={{0,8},{8,16},{16,24},{24,0},{1,9},{9,17},{17,25},{25,1},{2,10},{10... | collective-permute-start | bytes 2359304 | tf_op jit(solution)/shard_map/ppermute | solution.py:85
  258.2 217.7 %all-gather.8.cloned.1.call-start = ((), (), s32[]{:S(2)}) async-start(), calls=%async_computation.7 | async-start | bytes 7962624 | tf_op jit(solution)/shard_map/all_gather | solution.py:184
  260.5 36.6 %collective-permute-start.19 = (f32[256,1536]{1,0:T(8,128)S(1)}, f32[256,1536]{1,0:T(8,128)S(1)}, u32[]{:S(2)}, u32[]{:S(2)}) collective-permute-start(f32[256,1536]{1,0:T(8,128)S(1)} %add.561), channel_id=1, source_target_pairs={{0,2},{1,3},{2,0},{3,1},{4,6},{5,7},{6,4},{7,5},{8,10},{9,11},{10,... | collective-permute-start | bytes 4718600 | tf_op jit(solution)/shard_map/ppermute | solution.py:89
  269.0 30.4 %collective-permute-start.20 = (f32[256,1536]{1,0:T(8,128)}, f32[256,1536]{1,0:T(8,128)}, u32[]{:S(2)}, u32[]{:S(2)}) collective-permute-start(f32[256,1536]{1,0:T(8,128)} %get-tuple-element.679), channel_id=1, source_target_pairs={{0,1},{1,0},{2,3},{3,2},{4,5},{5,4},{6,7},{7,6},{8,9},{9,8},{10,11... | collective-permute-start | bytes 4718600 | tf_op jit(solution)/shard_map/ppermute | solution.py:89
  297.4 37.0 %collective-permute-start.22 = (f32[256,1536]{1,0:T(8,128)}, f32[256,1536]{1,0:T(8,128)S(1)}, u32[]{:S(2)}, u32[]{:S(2)}) collective-permute-start(f32[256,1536]{1,0:T(8,128)} %add.562), channel_id=1, source_target_pairs={{0,2},{1,3},{2,0},{3,1},{4,6},{5,7},{6,4},{7,5},{8,10},{9,11},{10,... | collective-permute-start | bytes 4718600 | tf_op jit(solution)/shard_map/ppermute | solution.py:89
  299.2 36.9 %collective-permute-start.23 = (f32[256,1536]{1,0:T(8,128)}, f32[256,1536]{1,0:T(8,128)S(1)}, u32[]{:S(2)}, u32[]{:S(2)}) collective-permute-start(f32[256,1536]{1,0:T(8,128)} %get-tuple-element.686), channel_id=1, source_target_pairs={{0,1},{1,0},{2,3},{3,2},{4,5},{5,4},{6,7},{7,6},{8,9},{9,8},{10,11... | collective-permute-start | bytes 4718600 | tf_op jit(solution)/shard_map/ppermute | solution.py:89
  366.6 367.9 %reduce-scatter.6.cloned.1.call-start = ((), (), s32[]{:S(2)}) async-start(), calls=%async_computation.8 | async-start | bytes 7962624 | tf_op jit(solution)/shard_map/reduce_scatter | solution.py:230
  366.7 36.0 %collective-permute-start.25 = (f32[256,1536]{1,0:T(8,128)}, f32[256,1536]{1,0:T(8,128)S(1)}, u32[]{:S(2)}, u32[]{:S(2)}) collective-permute-start(f32[256,1536]{1,0:T(8,128)} %add.566), channel_id=1, source_target_pairs={{0,2},{1,3},{2,0},{3,1},{4,6},{5,7},{6,4},{7,5},{8,10},{9,11},{10,... | collective-permute-start | bytes 4718600 | tf_op jit(solution)/shard_map/ppermute | solution.py:89
  403.0 41.8 %collective-permute-start.27 = (f32[256,1536]{1,0:T(8,128)}, f32[256,1536]{1,0:T(8,128)}, u32[]{:S(2)}, u32[]{:S(2)}) collective-permute-start(f32[256,1536]{1,0:T(8,128)} %add.570), channel_id=1, source_target_pairs={{0,2},{1,3},{2,0},{3,1},{4,6},{5,7},{6,4},{7,5},{8,10},{9,11},{10,... | collective-permute-start | bytes 4718600 | tf_op jit(solution)/shard_map/ppermute | solution.py:89
  535.2 429.5 %reduce-scatter.8.cloned.1.call-start = ((), (), s32[]{:S(2)}) async-start(), calls=%async_computation.9 | async-start | bytes 7962624 | tf_op jit(solution)/shard_map/reduce_scatter | solution.py:230
  535.2 37.1 %collective-permute-start.31 = (f32[256,1536]{1,0:T(8,128)}, f32[256,1536]{1,0:T(8,128)}, u32[]{:S(2)}, u32[]{:S(2)}) collective-permute-start(f32[256,1536]{1,0:T(8,128)} %add.595), channel_id=1, source_target_pairs={{0,2},{1,3},{2,0},{3,1},{4,6},{5,7},{6,4},{7,5},{8,10},{9,11},{10,... | collective-permute-start | bytes 4718600 | tf_op jit(solution)/shard_map/ppermute | solution.py:89
  574.5 41.4 %collective-permute-start.34 = (f32[256,1536]{1,0:T(8,128)}, f32[256,1536]{1,0:T(8,128)}, u32[]{:S(2)}, u32[]{:S(2)}) collective-permute-start(f32[256,1536]{1,0:T(8,128)} %add.596), channel_id=1, source_target_pairs={{0,2},{1,3},{2,0},{3,1},{4,6},{5,7},{6,4},{7,5},{8,10},{9,11},{10,... | collective-permute-start | bytes 4718600 | tf_op jit(solution)/shard_map/ppermute | solution.py:89
  618.5 36.8 %collective-permute-start.37 = (f32[256,1536]{1,0:T(8,128)}, f32[256,1536]{1,0:T(8,128)}, u32[]{:S(2)}, u32[]{:S(2)}) collective-permute-start(f32[256,1536]{1,0:T(8,128)} %add.598), channel_id=1, source_target_pairs={{0,2},{1,3},{2,0},{3,1},{4,6},{5,7},{6,4},{7,5},{8,10},{9,11},{10,... | collective-permute-start | bytes 4718600 | tf_op jit(solution)/shard_map/ppermute | solution.py:89
  657.5 40.9 %collective-permute-start.40 = (f32[256,1536]{1,0:T(8,128)}, f32[256,1536]{1,0:T(8,128)}, u32[]{:S(2)}, u32[]{:S(2)}) collective-permute-start(f32[256,1536]{1,0:T(8,128)} %add.601), channel_id=1, source_target_pairs={{0,2},{1,3},{2,0},{3,1},{4,6},{5,7},{6,4},{7,5},{8,10},{9,11},{10,... | collective-permute-start | bytes 4718600 | tf_op jit(solution)/shard_map/ppermute | solution.py:89
  734.6 426.4 %reduce-scatter.10.cloned.1.call-start = ((), (), s32[]{:S(2)}) async-start(), calls=%async_computation.10 | async-start | bytes 4423680 | tf_op jit(solution)/shard_map/reduce_scatter | solution.py:189
  735.6 36.8 %collective-permute-start.43 = (f32[256,1536]{1,0:T(8,128)}, f32[256,1536]{1,0:T(8,128)}, u32[]{:S(2)}, u32[]{:S(2)}) collective-permute-start(f32[256,1536]{1,0:T(8,128)} %add.604), channel_id=1, source_target_pairs={{0,2},{1,3},{2,0},{3,1},{4,6},{5,7},{6,4},{7,5},{8,10},{9,11},{10,... | collective-permute-start | bytes 4718600 | tf_op jit(solution)/shard_map/ppermute | solution.py:89
  774.3 58.1 %collective-permute-start.46 = (f32[256,1536]{1,0:T(8,128)S(1)}, f32[256,1536]{1,0:T(8,128)}, u32[]{:S(2)}, u32[]{:S(2)}) collective-permute-start(f32[256,1536]{1,0:T(8,128)S(1)} %add.607), channel_id=1, source_target_pairs={{0,2},{1,3},{2,0},{3,1},{4,6},{5,7},{6,4},{7,5},{8,10},{9,11},{10,... | collective-permute-start | bytes 4718600 | tf_op jit(solution)/shard_map/ppermute | solution.py:89
  786.3 49.3 %collective-permute-start.47 = (f32[256,1536]{1,0:T(8,128)}, f32[256,1536]{1,0:T(8,128)}, u32[]{:S(2)}, u32[]{:S(2)}) collective-permute-start(f32[256,1536]{1,0:T(8,128)} %get-tuple-element.923), channel_id=1, source_target_pairs={{0,1},{1,0},{2,3},{3,2},{4,5},{5,4},{6,7},{7,6},{8,9},{9,8},{10,11... | collective-permute-start | bytes 4718600 | tf_op jit(solution)/shard_map/ppermute | solution.py:89
  834.3 117.0 %collective-permute-start.50 = (f32[256,1536]{1,0:T(8,128)S(1)}, f32[256,1536]{1,0:T(8,128)S(1)}, u32[]{:S(2)}, u32[]{:S(2)}) collective-permute-start(f32[256,1536]{1,0:T(8,128)S(1)} %add.610), channel_id=1, source_target_pairs={{0,2},{1,3},{2,0},{3,1},{4,6},{5,7},{6,4},{7,5},{8,10},{9,11},{10,... | collective-permute-start | bytes 4718600 | tf_op jit(solution)/shard_map/ppermute | solution.py:89
  834.9 129.8 %collective-permute-start.52 = (f32[4,192,1152]{2,1,0:T(8,128)}, f32[4,192,1152]{2,1,0:T(8,128)}, u32[]{:S(2)}, u32[]{:S(2)}) collective-permute-start(f32[4,192,1152]{2,1,0:T(8,128)} %get-tuple-element.946), channel_id=1, source_target_pairs={{0,4},{4,0},{1,5},{5,1},{2,6},{6,2},{3,7},{7,3},{8,12},{12,8},{9,1... | collective-permute-start | bytes 10616840 | tf_op jit(solution)/shard_map/ppermute | solution.py:89
  867.8 49.2 %collective-permute-start.49 = (f32[8,512]{1,0:T(8,128)S(1)}, f32[8,512]{1,0:T(8,128)S(1)}, u32[]{:S(2)}, u32[]{:S(2)}) collective-permute-start(f32[8,512]{1,0:T(8,128)S(1)} %slice_bitcast_fusion.2), channel_id=1, source_target_pairs={{4,0},{5,1},{6,2},{7,3},{12,8},{13,9},{14,10},{15,11},{20,16},{21,... | collective-permute-start | bytes 49160 | tf_op jit(solution)/shard_map/ppermute | solution.py:80
  952.1 51.5 %collective-permute-start.55 = (f32[256,1536]{1,0:T(8,128)}, f32[256,1536]{1,0:T(8,128)}, u32[]{:S(2)}, u32[]{:S(2)}) collective-permute-start(f32[256,1536]{1,0:T(8,128)} %add.613), channel_id=1, source_target_pairs={{0,2},{1,3},{2,0},{3,1},{4,6},{5,7},{6,4},{7,5},{8,10},{9,11},{10,... | collective-permute-start | bytes 4718600 | tf_op jit(solution)/shard_map/ppermute | solution.py:89
  964.4 51.4 %collective-permute-start.56 = (f32[256,1536]{1,0:T(8,128)}, f32[256,1536]{1,0:T(8,128)}, u32[]{:S(2)}, u32[]{:S(2)}) collective-permute-start(f32[256,1536]{1,0:T(8,128)} %get-tuple-element.1011), channel_id=1, source_target_pairs={{0,1},{1,0},{2,3},{3,2},{4,5},{5,4},{6,7},{7,6},{8,9},{9,8},{10,11... | collective-permute-start | bytes 4718600 | tf_op jit(solution)/shard_map/ppermute | solution.py:89
  1006.2 36.5 %collective-permute-start.58 = (f32[256,1536]{1,0:T(8,128)S(1)}, f32[256,1536]{1,0:T(8,128)}, u32[]{:S(2)}, u32[]{:S(2)}) collective-permute-start(f32[256,1536]{1,0:T(8,128)S(1)} %add.616), channel_id=1, source_target_pairs={{0,2},{1,3},{2,0},{3,1},{4,6},{5,7},{6,4},{7,5},{8,10},{9,11},{10,... | collective-permute-start | bytes 4718600 | tf_op jit(solution)/shard_map/ppermute | solution.py:89
  1015.8 51.9 %collective-permute-start.59 = (f32[256,1536]{1,0:T(8,128)}, f32[256,1536]{1,0:T(8,128)}, u32[]{:S(2)}, u32[]{:S(2)}) collective-permute-start(f32[256,1536]{1,0:T(8,128)} %get-tuple-element.1041), channel_id=1, source_target_pairs={{0,1},{1,0},{2,3},{3,2},{4,5},{5,4},{6,7},{7,6},{8,9},{9,8},{10,11... | collective-permute-start | bytes 4718600 | tf_op jit(solution)/shard_map/ppermute | solution.py:89
  1044.4 208.3 %reduce-scatter.12.cloned.1.call-start = ((), (), s32[]{:S(2)}) async-start(), calls=%async_computation.11 | async-start | bytes 3932160 | tf_op jit(solution)/shard_map/reduce_scatter | solution.py:189
  1044.5 43.1 %collective-permute-start.64 = (f32[256,1536]{1,0:T(8,128)}, f32[256,1536]{1,0:T(8,128)}, u32[]{:S(2)}, u32[]{:S(2)}) collective-permute-start(f32[256,1536]{1,0:T(8,128)} %add.623), channel_id=1, source_target_pairs={{0,2},{1,3},{2,0},{3,1},{4,6},{5,7},{6,4},{7,5},{8,10},{9,11},{10,... | collective-permute-start | bytes 4718600 | tf_op jit(solution)/shard_map/ppermute | solution.py:89
  1045.1 39.6 %collective-permute-start.61 = (f32[1068,128]{1,0:T(8,128)}, f32[1068,128]{1,0:T(8,128)S(1)}, u32[]{:S(2)}, u32[]{:S(2)}) collective-permute-start(f32[1068,128]{1,0:T(8,128)} %pad_maximum_fusion.6), channel_id=1, source_target_pairs={{0,4},{4,0},{1,5},{5,1},{2,6},{6,2},{3,7},{7,3},{8,12},{12,8},{9,1... | collective-permute-start | bytes 1640456 | tf_op jit(solution)/shard_map/ppermute | solution.py:89
  1047.7 43.5 %collective-permute-start.65 = (f32[256,1536]{1,0:T(8,128)}, f32[256,1536]{1,0:T(8,128)}, u32[]{:S(2)}, u32[]{:S(2)}) collective-permute-start(f32[256,1536]{1,0:T(8,128)} %get-tuple-element.1074), channel_id=1, source_target_pairs={{0,1},{1,0},{2,3},{3,2},{4,5},{5,4},{6,7},{7,6},{8,9},{9,8},{10,11... | collective-permute-start | bytes 4718600 | tf_op jit(solution)/shard_map/ppermute | solution.py:89
  1090.4 70.6 %collective-permute-start.68 = (f32[4,192,1024]{2,1,0:T(8,128)S(1)}, f32[4,192,1024]{2,1,0:T(8,128)}, u32[]{:S(2)}, u32[]{:S(2)}) collective-permute-start(f32[4,192,1024]{2,1,0:T(8,128)S(1)} %copy-done.50), channel_id=1, source_target_pairs={{0,4},{4,0},{1,5},{5,1},{2,6},{6,2},{3,7},{7,3},{8,12},{12,8},{9,1... | collective-permute-start | bytes 9437192 | tf_op jit(solution)/shard_map/ppermute | solution.py:89
  1165.3 124.9 %reduce-scatter.14.cloned.1.call-start = ((), (), s32[]{:S(2)}) async-start(), calls=%async_computation.12 | async-start | bytes 1966080 | tf_op jit(solution)/shard_map/reduce_scatter | solution.py:189
  1166.6 36.0 %collective-permute-start.63 = (f32[256,1536]{1,0:T(8,128)S(1)}, f32[256,1536]{1,0:T(8,128)S(1)}, u32[]{:S(2)}, u32[]{:S(2)}) collective-permute-start(f32[256,1536]{1,0:T(8,128)S(1)} %copy-done.43), channel_id=1, source_target_pairs={{0,2},{1,3},{2,0},{3,1},{4,6},{5,7},{6,4},{7,5},{8,10},{9,11},{10,... | collective-permute-start | bytes 4718600 | tf_op jit(solution)/shard_map/ppermute | solution.py:89
  1168.2 32.6 %collective-permute-start.62 = (f32[1068,128]{1,0:T(8,128)}, f32[1068,128]{1,0:T(8,128)S(1)}, u32[]{:S(2)}, u32[]{:S(2)}) collective-permute-start(f32[1068,128]{1,0:T(8,128)} %add.635), channel_id=1, source_target_pairs={{0,8},{8,0},{16,24},{24,16},{1,9},{9,1},{17,25},{25,17},{2,10},{10... | collective-permute-start | bytes 1640456 | tf_op jit(solution)/shard_map/ppermute | solution.py:89
  1204.5 51.1 %collective-permute-start.75 = (f32[256,1536]{1,0:T(8,128)S(1)}, f32[256,1536]{1,0:T(8,128)}, u32[]{:S(2)}, u32[]{:S(2)}) collective-permute-start(f32[256,1536]{1,0:T(8,128)S(1)} %copy-done.42), channel_id=1, source_target_pairs={{0,2},{1,3},{2,0},{3,1},{4,6},{5,7},{6,4},{7,5},{8,10},{9,11},{10,... | collective-permute-start | bytes 4718600 | tf_op jit(solution)/shard_map/ppermute | solution.py:89
  1205.1 46.8 %collective-permute-start.72 = (f32[1068,128]{1,0:T(8,128)S(1)}, f32[1068,128]{1,0:T(8,128)S(1)}, u32[]{:S(2)}, u32[]{:S(2)}) collective-permute-start(f32[1068,128]{1,0:T(8,128)S(1)} %add.636), channel_id=1, source_target_pairs={{0,16},{8,24},{16,0},{24,8},{1,17},{9,25},{17,1},{25,9},{2,18},{10... | collective-permute-start | bytes 1640456 | tf_op jit(solution)/shard_map/ppermute | solution.py:89
  1207.7 45.0 %collective-permute-start.73 = (f32[4,192,512]{2,1,0:T(8,128)S(1)}, f32[4,192,512]{2,1,0:T(8,128)}, u32[]{:S(2)}, u32[]{:S(2)}) collective-permute-start(f32[4,192,512]{2,1,0:T(8,128)S(1)} %copy-done.91), channel_id=1, source_target_pairs={{0,4},{4,0},{1,5},{5,1},{2,6},{6,2},{3,7},{7,3},{8,12},{12,8},{9,1... | collective-permute-start | bytes 4718600 | tf_op jit(solution)/shard_map/ppermute | solution.py:89
  1217.1 38.5 %collective-permute-start.74 = (f32[12,128]{1,0:T(8,128)S(1)}, f32[12,128]{1,0:T(8,128)S(1)}, u32[]{:S(2)}, u32[]{:S(2)}) collective-permute-start(f32[12,128]{1,0:T(8,128)S(1)} %add.646), channel_id=1, source_target_pairs={{0,8},{8,0},{16,24},{24,16},{1,9},{9,1},{17,25},{25,17},{2,10},{10... | collective-permute-start | bytes 18440 | tf_op jit(solution)/shard_map/ppermute | solution.py:89
  (147 other events, 2009.7 us)
Sparse Core Ops, SparseCore 0:
  10.2 160.3 all-gather.3
  258.3 108.2 all-gather.5
  368.8 106.9 all-gather.7
  535.3 127.2 reduce-scatter.5
  734.7 126.7 reduce-scatter.7
  1044.5 67.6 reduce-scatter.9
  1165.4 80.4 reduce-scatter.11
  1257.5 32.6 reduce-scatter.13

commit v2 on v1

--- a/solution.py
+++ b/solution.py
@@ -184,50 +184,47 @@
     return lax.all_gather(block, ("shard", "ctx"), axis=0, tiled=True)
 
 
-def over_shard(rows):
-    shards, count, width = rows.shape
-    return lax.psum_scatter(
-        rows.reshape(shards * count, width), "shard", scatter_dimension=0, tiled=True
-    )
-
-
 class Scatter:
-    def __init__(self, kept, sent, order, earlier):
-        self.kept, self.sent, self.order, self.earlier = kept, sent, order, earlier
-        self.rows = kept.v.shape[1]
+    def __init__(self, kept, sent, order):
+        self.kept, self.sent, self.order = kept, sent, order
+        self.shards = lax.axis_size("shard")
 
     def start_ctx(self):
         self.arriving = self.order.send(swapped, self.sent, "ctx", 1)
 
-    def take_turn(self):
-        if self.earlier:
-            self.order.wait(self.earlier[-1])
-
-    def end_ctx(self):
-        self.take_turn()
-        both = self.order.step(lambda one, two: one + two, self.kept, self.arriving)
-        self.result = Box(over_shard(self.order.gate(both)[0]))
-        self.earlier.append(self.result)
-
     def start_shard(self):
-        self.take_turn()
-        both = self.order.step(
-            lambda one, two: jnp.concatenate([one, two], axis=1), self.kept, self.sent
-        )
-        self.both = Box(over_shard(self.order.gate(both)[0]))
-        self.earlier.append(self.both)
-
-    def end_shard(self):
-        rows = self.rows
-        sent = self.order.step(lambda both: both[rows:], self.both)
-        self.arriving = self.order.send(swapped, sent, "ctx", 1)
-        self.result = self.order.step(
-            lambda both, other: both[:rows] + other, self.both, self.arriving
-        )
-
-
-def scatter_plain(total):
-    return lax.psum_scatter(total, ("shard", "ctx"), scatter_dimension=0, tiled=True)
+        z = lax.axis_index("shard")
+        parts = self.order.step(
+            lambda kept, other: [
+                lax.dynamic_index_in_dim(kept, (z + step) % self.shards, 0, keepdims=False)
+                + lax.dynamic_index_in_dim(other, (z + step) % self.shards, 0, keepdims=False)
+                for step in range(self.shards)
+            ],
+            self.kept, self.arriving,
+        )
+        self.mine = parts[0]
+        self.parts = [
+            self.order.send(rotated, parts[step], "shard", step) for step in range(1, self.shards)
+        ]
+
+    def result(self):
+        return self.order.step(lambda *parts: sum(parts[1:], parts[0]), self.mine, *self.parts)
+
+
+class Unsplit:
+    def __init__(self, total):
+        self.kept = total
+
+    def start_ctx(self):
+        pass
+
+    def start_shard(self):
+        pass
+
+    def result(self):
+        return Box(
+            lax.psum_scatter(self.kept.v, ("shard", "ctx"), scatter_dimension=0, tiled=True)
+        )
 
 
 class TpSum:
@@ -556,19 +553,20 @@
     (chunk, depth), width = lefts[0].shape, rights[0].shape[1]
     shards = lax.axis_size("shard")
     rows = depth // (2 * shards)
+    step = 2 * rows if split else 384 if depth % 384 == 0 else depth
     span = lax.axis_index("ctx").astype(jnp.int32).reshape(1)
     if split:
         out_specs = [pl.BlockSpec((1, rows, wide * width), lambda i, span: (i, 0, 0))] * 2
         out_shape = [shaped(shards, rows, wide * width)] * 2
     else:
-        out_specs = [pl.BlockSpec((2 * rows, wide * width), lambda i, span: (i, 0))]
+        out_specs = [pl.BlockSpec((step, wide * width), lambda i, span: (i, 0))]
         out_shape = [shaped(depth, wide * width)]
     return pl.pallas_call(
         functools.partial(product_kernel, count=count, wide=wide, split=split),
         grid_spec=pltpu.PrefetchScalarGridSpec(
             num_scalar_prefetch=1,
-            grid=(shards,),
-            in_specs=[pl.BlockSpec((chunk, 2 * rows), lambda i, span: (0, i))] * count
+            grid=(depth // step,),
+            in_specs=[pl.BlockSpec((chunk, step), lambda i, span: (0, i))] * count
             + [
                 pl.BlockSpec(
                     (chunk, width), lambda i, span: (0, 0), pipeline_mode=pl.Buffered(1)
@@ -583,6 +581,12 @@
     )(span, *lefts, *rights)
 
 
+def unwritten(rows, width):
+    return pl.pallas_call(
+        lambda ref: None, out_specs=pl.BlockSpec(memory_space=pl.ANY), out_shape=shaped(rows, width)
+    )()
+
+
 def dot_parts(left_high, left_low, right_high, right_low, dims):
     def part(one, two):
         return lax.dot_general(one, two, (dims, ((), ())), preferred_element_type=F32)
@@ -614,7 +618,7 @@
     sent_ref[...] = jnp.where(first, high, low)
 
 
-def run_across(lefts, rights, chunk, rows):
+def run_across(lefts, rights, columns, chunk, rows):
     count, depth = len(lefts), rights[0].shape[0]
     step = 512 if depth % 512 == 0 else depth
     side = (lax.axis_index("tp") % 2).astype(jnp.int32).reshape(1)
@@ -626,7 +630,10 @@
             num_scalar_prefetch=1,
             grid=(depth // step,),
             in_specs=[pl.BlockSpec((rows, w), lambda i, side: (chunk, 0)) for w in widths]
-            + [pl.BlockSpec((step, w), lambda i, side: (i, 0)) for w in widths],
+            + [
+                pl.BlockSpec((step, w), lambda i, side, column=column: (i, column))
+                for w, column in zip(widths, columns)
+            ],
             out_specs=[half, half],
             scratch_shapes=[pltpu.VMEM((rows, w), BF16) for w in widths for _ in range(2)],
         ),
@@ -694,36 +701,29 @@
     chunk_list = list(range(chunks))
     scattered = []
 
-    def weight_grad(lefts, rights, wide=1, split=True):
+    def weight_grad(lefts, rights, wide=1):
         count = len(lefts)
+        return order.step(
+            lambda *a: run_product(a[:count], a[count:], wide, False)[0], *lefts, *rights
+        )
+
+    def split_grad(lefts, rights, wide=1):
         if not two_level:
-            total = order.step(
-                lambda *a: matmul_tn(
-                    jnp.concatenate(a[:count]),
-                    jnp.concatenate(a[count:], axis=1 if wide > 1 else 0),
-                ),
-                *lefts, *rights,
-            )
-            return Box(scatter_plain(total.v))
-        out = order.step(
-            lambda *a: run_product(a[:count], a[count:], wide, split), *lefts, *rights
-        )
-        if split:
-            return Scatter(*out, order, scattered)
+            return Unsplit(weight_grad(lefts, rights, wide))
+        count = len(lefts)
+        kept, sent = order.step(
+            lambda *a: run_product(a[:count], a[count:], wide, True), *lefts, *rights
+        )
+        return Scatter(kept, sent, order)
+
+    def scatter(total, axes):
         if scattered:
             order.wait(scattered[-1])
-        scattered.append(Box(scatter_plain(order.gate(out[0])[0])))
+        total = order.gate(total)[0]
+        scattered.append(Box(lax.psum_scatter(total, axes, scatter_dimension=0, tiled=True)))
         return scattered[-1]
 
-    def start_ctx(grad):
-        if isinstance(grad, Scatter):
-            grad.start_ctx()
-
-    def end_ctx(grad):
-        if isinstance(grad, Scatter):
-            grad.end_ctx()
-            return grad.result
-        return grad
+    everywhere = ("shard", "ctx")
 
     flat_in = inputs.reshape(row_count, width_model)
     flat_cot = cotangent.reshape(row_count, width_model)
@@ -741,12 +741,14 @@
     turns = lax.axis_size("shard") - 1
     direct = two_level and turns == 3 and chunks == 4
 
-    def partial_sum(lefts, weights, c):
-        kept, sent = order.step(
-            lambda *a: run_across(a[: len(lefts)], a[len(lefts) :], c, chunk_rows),
+    def partial(lefts, weights, c, columns=(0, 0)):
+        return order.step(
+            lambda *a: run_across(a[: len(lefts)], a[len(lefts) :], columns, c, chunk_rows),
             *lefts, *weights,
         )
-        return TpSum(kept, sent, order)
+
+    def partial_sum(*args):
+        return TpSum(*partial(*args), order)
 
     def gathered(block, *earlier):
         order.wait(*earlier)
@@ -879,7 +881,7 @@
         def place(rows, kept, arriving, mask, block_out=None):
             rows = (rows + ffn_sums[c].rows(kept, arriving)) * rows_of(mask, c)
             if block_out is None:
-                block_out = jnp.zeros((row_count, width_model), F32)
+                block_out = unwritten(row_count, width_model)
             return lax.dynamic_update_slice(block_out, rows, (c * chunk_rows, 0))
 
         block_out = order.step(
@@ -909,11 +911,13 @@
         )
         grad_mixed[c] = order.step(matmul, grad_after_mix[c], out_weight)
 
+    rest = chunk_list[2:]
     start_ffn(0)
     start_ffn(1)
     ffn_sums[0].cross()
     ffn_sums[1].cross()
-    grad_fd = weight_grad(grad_result, hidden, split=False)
+    fd_product = weight_grad(grad_result, hidden)
+    grad_fd = scatter(fd_product, everywhere)
     run_hidden(3)
     start_back(3)
     ffn_sums[0].share()
@@ -932,7 +936,8 @@
     take_back(3)
     start_back(0)
     back_sums[2].share()
-    grad_fg = weight_grad(normed_two, grad_pre, split=False)
+    fg_product = weight_grad(normed_two, grad_pre)
+    grad_fg = scatter(fg_product, everywhere)
     back_sums[0].cross()
     take_back(2)
     start_ffn(2)
@@ -940,8 +945,8 @@
     start_ffn(3)
     ffn_sums[2].cross()
     take_back(1)
-    grad_fu = weight_grad(normed_two, grad_up)
-    start_ctx(grad_fu)
+    fu_product = weight_grad(normed_two, grad_up)
+    ffn_sums[2].share()
     back_sums[0].share()
     ffn_sums[3].cross()
     take_back(0)
@@ -950,7 +955,10 @@
         lambda pre, state, rate, table, *mixed: run_backward(mixed, pre, state, rate, table),
         gate_pre, rec_state, a_rate, table, *grad_mixed,
     )
+    ffn_sums[3].share()
     incoming = Box(carried_in(back_pair.v[0], back_pair.v[1], -1))
+    order.wait(incoming)
+    grad_fu = scatter(fu_product, everywhere)
     grad_branch, head, sums, grad_gates = order.step(
         run_gradient,
         suffix, local_adjoint, conv_out, a_rate, i_rate, rec_state, branch, incoming, entry,
@@ -969,7 +977,9 @@
     one_sums = [None] * chunks
 
     def start_one(c):
-        one_sums[c] = partial_sum([grad_branch, grad_gate_pre], [rec_weight, gbr_weight], c)
+        one_sums[c] = partial_sum(
+            [grad_branch, grad_gate_pre], [rec_weight, gbr_weight], c
+        )
 
     input_grad = None
 
@@ -982,7 +992,7 @@
                 one_sums[c].rows(kept, arriving), rows_of(after, c) * inv, inv, gain
             )
             if grads is None:
-                grads = jnp.zeros((row_count, width_model), F32)
+                grads = unwritten(row_count, width_model)
             return lax.dynamic_update_slice(grads, rows + from_one, (c * chunk_rows, 0))
 
         input_grad = order.step(
@@ -1005,83 +1015,74 @@
         )
 
     start_one(0)
-    ffn_sums[2].share()
     start_one(1)
     one_sums[0].cross()
-    grad_fu = end_ctx(grad_fu)
-    take_ffn(2)
     grad_branch = order.step(tail_rows, grad_branch, right_edges, conv_weight)
-    grad_recs = weight_grad([normed_one], [grad_branch, grad_gate_pre], wide=2)
-    rec_parts = grad_recs
-    start_ctx(grad_recs)
-    ffn_sums[3].share()
     start_one(2)
     one_sums[1].cross()
-    take_ffn(3)
+    start_one(3)
+    one_sums[2].cross()
     small = order.step(
         small_parts, sums, head, left_edges, grad_gates, lambda_param, *norm_two_sums
     )
     small = SmallSum(small, order, ("ctx", "shard"))
     small.advance()
-    start_one(3)
+    one_sums[3].cross()
+    recs = split_grad([normed_one], [grad_branch, grad_gate_pre], wide=2)
+    recs.start_ctx()
+    outs = split_grad(
+        grad_after_mix, order.step(lambda rows: [rows_of(rows, c) for c in chunk_list], mixed_rows)
+    )
+    outs.start_ctx()
+    for c in rest:
+        take_ffn(c)
+    block_out = block_out.v.reshape(seqs_here, span_len, width_model)
+
+    def gain_sums(gain, rec_weight, gbr_weight, kept, sent=None):
+        def rows_sum(grads, which):
+            total = 0.0
+            for place, weight in enumerate((rec_weight, gbr_weight)):
+                if which is not None:
+                    weight = weight.reshape(-1, 2, grads.shape[1], width_rec)
+                    weight = lax.dynamic_index_in_dim(weight, which, 1, keepdims=False)
+                columns = slice(place * width_rec, (place + 1) * width_rec)
+                total = total + jnp.sum(grads[..., columns] * weight, axis=-1)
+            return total
+
+        if sent is None:
+            total = rows_sum(kept, None)
+        else:
+            span = lax.axis_index("ctx")
+            kept, sent = rows_sum(kept, span), rows_sum(sent, 1 - span)
+            total = jnp.stack(
+                [jnp.where(span == 0, kept, sent), jnp.where(span == 0, sent, kept)], axis=1
+            ).reshape(-1)
+        return (total / gain).reshape(-1, 128)
+
+    norm_one_sum = order.step(
+        gain_sums, rec_norm, rec_weight, gbr_weight, recs.kept,
+        *([recs.sent] if two_level else []),
+    )
+    tiny = SmallSum(norm_one_sum, order, ("tp", "ctx", "shard"))
+    order.wait(grad_fu)
     one_sums[0].share()
-    grad_out_proj = weight_grad(
-        grad_after_mix, order.step(lambda rows: [rows_of(rows, c) for c in chunk_list], mixed_rows)
-    )
-    one_sums[2].cross()
+    one_sums[1].share()
+    recs.start_shard()
+    one_sums[2].share()
+    one_sums[3].share()
+    outs.start_shard()
+    small.advance()
+    grad_recs = recs.result()
+    tiny.advance()
     take_one(0)
+    tiny.advance()
+    take_one(1)
     small.advance()
-    block_out = block_out.v.reshape(seqs_here, span_len, width_model)
-
-    if two_level:
-        span = lax.axis_index("ctx")
-
-        def gain_sums(kept, sent, gain, rec_weight, gbr_weight):
-            def rows_sum(grads, which):
-                total = 0.0
-                for place, weight in enumerate((rec_weight, gbr_weight)):
-                    split = weight.reshape(turns + 1, 2, -1, width_rec)
-                    split = lax.dynamic_index_in_dim(split, which, 1, keepdims=False)
-                    grad = grads[:, :, place * width_rec : (place + 1) * width_rec]
-                    total = total + jnp.sum(grad * split, axis=2)
-                return total
-
-            kept, sent = rows_sum(kept, span), rows_sum(sent, 1 - span)
-            both = jnp.stack(
-                [jnp.where(span == 0, kept, sent), jnp.where(span == 0, sent, kept)], axis=1
-            )
-            return (both.reshape(-1) / gain).reshape(-1, 128)
-
-        norm_one_sum = order.step(
-            gain_sums, rec_parts.kept, rec_parts.sent, rec_norm, rec_weight, gbr_weight
-        )
-    else:
-        def gain_sums(grads, more, normed, gain, first, second):
-            back = matmul_nt(grads, first) + matmul_nt(more, second)
-            return (jnp.sum(back * normed, axis=0) / gain).reshape(-1, 128)
-
-        norm_one_sum = order.step(
-            gain_sums, grad_branch, grad_gate_pre, normed_one, rec_norm, rec_weight, gbr_weight
-        )
-    tiny = SmallSum(norm_one_sum, order, ("tp", "ctx", "shard"))
-    one_sums[1].share()
-    tiny.advance()
-    one_sums[3].cross()
-    take_one(1)
-    tiny.advance()
-    grad_recs = end_ctx(grad_recs)
-    start_ctx(grad_out_proj)
-    small.advance()
-    one_sums[2].share()
     tiny.advance()
     take_one(2)
     tiny.advance()
-    small.advance()
-    grad_out_proj = end_ctx(grad_out_proj)
-    tiny.advance()
-    one_sums[3].share()
-    tiny.advance()
     take_one(3)
+    grad_out_proj = outs.result()
     for left in (small, tiny):
         while left.advance():
             pass

time: 1310 us -> 1240 us (0.947)
  waiting for transfers between devices: 394 us -> 348 us
  local copies, waits for them, and re-layouts: 84.5 us -> 65.7 us
    ppermute x9 -> x15, waiting for transfers between devices: 85.7 us -> 132 us  [rotated(): lax.ppermute(block, axis, [(i, (i + distance) % count) for i in range(cou...]
    ppermute x4, waiting for transfers between devices: 47.9 us -> 7.01 us  [passed_along(): return lax.ppermute(block, axis, route)]
    ppermute x65 -> x64, waiting for transfers between devices: 227 us -> 190 us  [swapped(): lax.ppermute(block, axis, [(i, i ^ bit) for i in range(lax.axis_size(axis...]
    reduce_scatter x5 -> x3, waiting for transfers between devices: 14.8 us -> 0.02 us  [scatter(): lax.psum_scatter(total, axes, scatter_dimension=0, tiled=True)]
    dynamic_update_slice x2 -> x0, local copies, waits for them, and re-layouts: 14.5 us -> none  [the longest x1 8.06 us: back(): return lax.dynamic_update_slice(grads, rows + from_one, (c * chunk_rows, 0))]
    ppermute x65 -> x64, starting transfers between devices: 48.3 us -> 41.3 us  [swapped(): lax.ppermute(block, axis, [(i, i ^ bit) for i in range(lax.axis_size(axis...]
    unnamed x209 -> x215, local copies, waits for them, and re-layouts: 37.8 us -> 38.2 us
  transfers between devices with their start and end apart: 86 -> 89, of which waited for: 28 -> 34; matrix products, arithmetic and copies ran while one was open for 29% -> 29% of each run, Pallas kernels for 26% -> 27%
where the time goes in v2:
time: 1240 us; the launch traced here: 1230 us
  Pallas kernels  384 us (31%)
  waiting for transfers between devices  348 us (28%)
  other arithmetic  172 us (14%)
  matrix products  167 us (13%)
  starting transfers between devices  77.7 us (6%)
  local copies, waits for them, and re-layouts  65.7 us (5%)
  between operations  16.9 us (1%)
    ppermute x64, waiting for transfers between devices, swapped(): lax.ppermute(block, axis, [(i, i ^ bit) for i in range(lax.axis_size(axis...  190 us
    pallas_call x16, Pallas kernels, run_across(): pl.pallas_call(functools.partial(across_kernel, count=count), grid_spec=p...  181 us
    dot_general x18, matrix products, matmul(): return jnp.dot(left, right, precision=HIGH, preferred_element_type=F32)  167 us
    pallas_call x5, Pallas kernels, run_product(): pl.pallas_call(functools.partial(product_kernel, count=count, wide=wide,...  142 us
    ppermute x15, waiting for transfers between devices, rotated(): lax.ppermute(block, axis, [(i, (i + distance) % count) for i in range(cou...  132 us
    ppermute x64, starting transfers between devices, swapped(): lax.ppermute(block, axis, [(i, i ^ bit) for i in range(lax.axis_size(axis...  41.3 us
    unnamed x215, local copies, waits for them, and re-layouts  38.2 us
    add x16, other arithmetic, cross(): one + two  32 us
  transfers between devices with their start and end apart: 89, of which 34 were waited for; matrix products, arithmetic and copies ran while one was open for 29% of the time, Pallas kernels for 27%

profile of v2, /device:TPU:0, one launch (start us, length us, event | category | flops | bytes accessed | tf_op | source)
XLA Modules:
  0.0 1231.8 jit_solution(14488907717107000931)
XLA Ops:
  23.0 21.4 %collective-permute-done.1 = f32[192,512]{1,0:T(8,128)} collective-permute-done((f32[192,512]{1,0:T(8,128)}, f32[192,512]{1,0:T(8,128)}, u32[]{:S(2)}, u32[]{:S(2)}) %collective-permute-start.1) | collective-permute-done | bytes 393248 | tf_op jit(solution)/shard_map/ppermute | solution.py:85
  52.2 18.1 %collective-permute-done.2 = f32[192,512]{1,0:T(8,128)S(1)} collective-permute-done((f32[192,512]{1,0:T(8,128)}, f32[192,512]{1,0:T(8,128)S(1)}, u32[]{:S(2)}, u32[]{:S(2)}) %collective-permute-start.2) | collective-permute-done | bytes 393248 | tf_op jit(solution)/shard_map/ppermute | solution.py:85
  81.4 10.5 multiply_multiply_fusion.refs_0_
  95.0 10.9 collective-permute-done.7
  106.0 12.4 %collective-permute-done.8 = f32[192,512]{1,0:T(8,128)S(1)} collective-permute-done((f32[192,512]{1,0:T(8,128)S(1)}, f32[192,512]{1,0:T(8,128)S(1)}, u32[]{:S(2)}, u32[]{:S(2)}) %collective-permute-start.8) | collective-permute-done | bytes 393248 | tf_op jit(solution)/shard_map/ppermute | solution.py:89
  120.2 14.4 %fusion.42.branch_ref = f32[2048,512]{1,0:T(8,128)S(1)} fusion(f32[2048,1536]{1,0:T(8,128)} %multiply_multiply_fusion.refs_0_, f32[1536,512]{1,0:T(8,128)S(1)} %bitcast.233), kind=kOutput, calls=%fused_computation.222 | convolution fusion | flops 9663676416 | bytes 19922944 | tf_op jit(solution)/shard_map/dot_general | solution.py:21
  134.6 20.8 %collective-permute-done.10 = f32[2,192,512]{2,1,0:T(8,128)S(1)} collective-permute-done((f32[2,192,512]{2,1,0:T(8,128)}, f32[2,192,512]{2,1,0:T(8,128)S(1)}, u32[]{:S(2)}, u32[]{:S(2)}) %collective-permute-start.10) | collective-permute-done | bytes 786464 | tf_op jit(solution)/shard_map/ppermute | solution.py:85
  170.8 9.1 collective-permute-done.11
  181.9 11.5 fusion.43.pre_ref
  200.2 18.1 %shard_map.306 = (f32[2048,512]{1,0:T(8,128)}, f32[2048,512]{1,0:T(8,128)}, f32[2048,512]{1,0:T(8,128)}, f32[2048,512]{1,0:T(8,128)}, f32[2048,512]{1,0:T(8,128)}, /*index=5*/f32[2,8,512]{2,1,0:T(8,128)}) custom-call(f32[2048,512]{1,0:T(8,128)} %copy-done.41, f32[8,512]{1,0:T(8,128)} %pad.6.edge_ref, f32[4,512]{1,0:T(4,128)} %taps_ref.1, ...), custom_call_target="tpu_custom_call" | custom-call | tf_op jit(solution)/shard_map/pallas_call | solution.py:451
  313.9 17.3 %collective-permute-done.22 = f32[256,1536]{1,0:T(8,128)S(1)} collective-permute-done((f32[256,1536]{1,0:T(8,128)}, f32[256,1536]{1,0:T(8,128)S(1)}, u32[]{:S(2)}, u32[]{:S(2)}) %collective-permute-start.22) | collective-permute-done | bytes 1572896 | tf_op jit(solution)/shard_map/ppermute | solution.py:89
  342.5 8.6 fusion.45
  351.1 12.2 all-gather.6.cloned.1.call-done.refs_3_
  364.9 12.8 %add_multiply_fusion.3 = (f32[512,1152]{1,0:T(8,128)}, f32[512,1152]{1,0:T(8,128)}, f32[512,1152]{1,0:T(8,128)}) fusion(f32[512,1152]{1,0:T(8,128)} %fusion.44, f32[512,1536]{1,0:T(8,128)S(1)} %multiply_multiply_fusion.5.refs_0_, f32[1536,1152]{1,0:T(8,128)} %all-gather.6.cloned.1.call-done.refs_3_), kind=kOutput, calls=%fused_computation.76 | convolution fusion | flops 5447024640 | bytes 19660800 | tf_op jit(solution)/shard_map/dot_general | solution.py:21
  377.7 21.6 %collective-permute-done.25 = f32[256,1536]{1,0:T(8,128)S(1)} collective-permute-done((f32[256,1536]{1,0:T(8,128)}, f32[256,1536]{1,0:T(8,128)S(1)}, u32[]{:S(2)}, u32[]{:S(2)}) %collective-permute-start.25) | collective-permute-done | bytes 1572896 | tf_op jit(solution)/shard_map/ppermute | solution.py:89
  401.2 12.5 %add_multiply_fusion.2 = (f32[512,1152]{1,0:T(8,128)}, f32[512,1152]{1,0:T(8,128)}, f32[512,1152]{1,0:T(8,128)}) fusion(f32[512,1152]{1,0:T(8,128)} %fusion.45, f32[512,1536]{1,0:T(8,128)S(1)} %copy-done.36, f32[1536,1152]{1,0:T(8,128)S(1)} %copy-done), kind=kOutput, calls=%fused_computation.74 | convolution fusion | flops 5447024640 | bytes 19660800 | tf_op jit(solution)/shard_map/dot_general | solution.py:21
  429.0 12.5 %add_multiply_fusion.1 = (f32[512,1152]{1,0:T(8,128)}, f32[512,1152]{1,0:T(8,128)}, f32[512,1152]{1,0:T(8,128)}) fusion(f32[512,1152]{1,0:T(8,128)} %fusion.46, f32[512,1536]{1,0:T(8,128)} %copy-done.37, f32[1536,1152]{1,0:T(8,128)S(1)} %copy-done), kind=kOutput, calls=%fused_computation.72 | convolution fusion | flops 5447024640 | bytes 19660800 | tf_op jit(solution)/shard_map/dot_general | solution.py:21
  456.5 10.3 add_multiply_fusion
  472.5 10.7 shard_map.311
  483.2 10.6 shard_map.312
  498.9 32.9 %shard_map.313 = f32[1536,1152]{1,0:T(8,128)} custom-call(s32[1]{0:T(128)} %bitcast.span_ref, f32[512,1536]{1,0:T(8,128)} %slice_multiply_fusion.7.refs_0_, f32[512,1536]{1,0:T(8,128)} %slice_multiply_fusion.6.refs_1_, f32[512,1536]{1,0:T(8,128)} %slice_multiply_fusion.5.refs_2_, f32[512,1536]{1,0:T(8,128)} %slice_multiply_fusion.4.refs_3_, ...), custom_call_target="tpu_custom_call" | custom-call | tf_op jit(solution)/shard_map/pallas_call | solution.py:564
  533.7 12.8 %fusion.37 = (f32[512,1152]{1,0:T(8,128)}, f32[512,1152]{1,0:T(8,128)}) fusion(f32[512,1152]{1,0:T(8,128)} %get-tuple-element.831, f32[512,1152]{1,0:T(8,128)} %get-tuple-element.830, f32[512,1536]{1,0:T(8,128)S(1)} %copy-done.38, f32[1536,1152]{1,0:T(8,128)} %all-gather.8.cloned.1.call-done.refs_1_), kind=kOutput, calls=%fused_computation.217 | convolution fusion | flops 5436997632 | bytes 19660800 | tf_op jit(solution)/shard_map/dot_general | solution.py:21
  546.5 18.5 %shard_map.314 = (f32[256,1536]{1,0:T(8,128)}, f32[256,1536]{1,0:T(8,128)}) custom-call(s32[1]{0:T(128)} %bitcast.1.side_ref, f32[512,1152]{1,0:T(8,128)} %get-tuple-element.933.refs_0_.refs_7_, f32[512,1152]{1,0:T(8,128)} %get-tuple-element.981.refs_1_.refs_7_, f32[1536,1152]{1,0:T(8,128)} %all-gather.4.cloned.1.call-done.refs_2_, ...), custom_call_target="tpu_custom_call" | custom-call | tf_op jit(solution)/shard_map/pallas_call | solution.py:627
  572.2 12.5 %fusion.36 = (f32[512,1152]{1,0:T(8,128)}, f32[512,1152]{1,0:T(8,128)}) fusion(f32[512,1152]{1,0:T(8,128)} %get-tuple-element.846, f32[512,1152]{1,0:T(8,128)} %get-tuple-element.845, f32[512,1536]{1,0:T(8,128)S(1)} %copy-done.33, f32[1536,1152]{1,0:T(8,128)} %all-gather.8.cloned.1.call-done.refs_1_), kind=kOutput, calls=%fused_computation.216 | convolution fusion | flops 5436997632 | bytes 19660800 | tf_op jit(solution)/shard_map/dot_general | solution.py:21
  592.4 19.6 %shard_map.315 = (f32[256,1536]{1,0:T(8,128)}, f32[256,1536]{1,0:T(8,128)}) custom-call(s32[1]{0:T(128)} %bitcast.1.side_ref, f32[512,1152]{1,0:T(8,128)} %get-tuple-element.932.refs_0_.refs_6_, f32[512,1152]{1,0:T(8,128)} %get-tuple-element.980.refs_1_.refs_6_, f32[1536,1152]{1,0:T(8,128)} %all-gather.4.cloned.1.call-done.refs_2_, ...), custom_call_target="tpu_custom_call" | custom-call | tf_op jit(solution)/shard_map/pallas_call | solution.py:627
  616.1 10.5 fusion.35
  631.9 18.5 %shard_map.316 = (f32[256,1536]{1,0:T(8,128)}, f32[256,1536]{1,0:T(8,128)}) custom-call(s32[1]{0:T(128)} %bitcast.1.side_ref, f32[512,1152]{1,0:T(8,128)} %get-tuple-element.931.refs_0_.refs_5_, f32[512,1152]{1,0:T(8,128)} %get-tuple-element.979.refs_1_.refs_5_, f32[1536,1152]{1,0:T(8,128)} %all-gather.4.cloned.1.call-done.refs_2_, ...), custom_call_target="tpu_custom_call" | custom-call | tf_op jit(solution)/shard_map/pallas_call | solution.py:627
  655.2 10.4 fusion.34
  676.9 18.3 %shard_map.317 = (f32[256,1536]{1,0:T(8,128)}, f32[256,1536]{1,0:T(8,128)}) custom-call(s32[1]{0:T(128)} %bitcast.1.side_ref, f32[512,1152]{1,0:T(8,128)} %get-tuple-element.930.refs_0_.refs_4_, f32[512,1152]{1,0:T(8,128)} %get-tuple-element.978.refs_1_.refs_4_, f32[1536,1152]{1,0:T(8,128)} %all-gather.4.cloned.1.call-done.refs_2_, ...), custom_call_target="tpu_custom_call" | custom-call | tf_op jit(solution)/shard_map/pallas_call | solution.py:627
  698.4 33.1 %shard_map.318 = f32[1536,1152]{1,0:T(8,128)} custom-call(s32[1]{0:T(128)} %bitcast.span_ref, f32[512,1536]{1,0:T(8,128)} %copy-done.32, f32[512,1536]{1,0:T(8,128)} %copy-done.35, f32[512,1536]{1,0:T(8,128)} %copy-done.37, f32[512,1536]{1,0:T(8,128)} %copy-done.40, f32[512,1152]{1,0:T(8,128)} %get-tuple-element.930.refs_0_.refs_4_, ...), custom_call_target="tpu_custom_call" | custom-call | tf_op jit(solution)/shard_map/pallas_call | solution.py:564
  748.0 11.0 shard_map.319
  759.1 9.8 collective-permute-done.43
  769.8 10.5 shard_map.320
  793.4 33.3 %shard_map.321 = f32[1536,1152]{1,0:T(8,128)} custom-call(s32[1]{0:T(128)} %bitcast.span_ref, f32[512,1536]{1,0:T(8,128)} %copy-done.32, f32[512,1536]{1,0:T(8,128)} %copy-done.35, f32[512,1536]{1,0:T(8,128)} %copy-done.37, f32[512,1536]{1,0:T(8,128)} %copy-done.40, f32[512,1152]{1,0:T(8,128)} %get-tuple-element.978.refs_1_.refs_4_, ...), custom_call_target="tpu_custom_call" | custom-call | tf_op jit(solution)/shard_map/pallas_call | solution.py:564
  826.7 13.3 %collective-permute-done.46 = f32[256,1536]{1,0:T(8,128)} collective-permute-done((f32[256,1536]{1,0:T(8,128)}, f32[256,1536]{1,0:T(8,128)}, u32[]{:S(2)}, u32[]{:S(2)}) %collective-permute-start.46) | collective-permute-done | bytes 1572896 | tf_op jit(solution)/shard_map/ppermute | solution.py:89
  857.4 18.7 %shard_map.322 = (f32[2048,512]{1,0:T(8,128)}, f32[2048,512]{1,0:T(8,128)}, f32[2048,512]{1,0:T(8,128)}, f32[2,8,512]{2,1,0:T(8,128)}) custom-call(f32[2048,512]{1,0:T(8,128)} %fusion.43.pre_ref, f32[2048,512]{1,0:T(8,128)} %get-tuple-element.1035.state_ref.before_ref, f32[2048,512]{1,0:T(8,128)} %get-tuple-element.1033.a_ref, ...), custom_call_target="tpu_custom_call" | custom-call | tf_op jit(solution)/shard_map/pallas_call | solution.py:476
  891.1 23.9 %shard_map.323 = (f32[2048,512]{1,0:T(8,128)}, f32[8,512]{1,0:T(8,128)}, f32[8,512]{1,0:T(8,128)}, f32[4,128,256]{2,1,0:T(8,128)}) custom-call(f32[2048,512]{1,0:T(8,128)} %get-tuple-element.1030.suffix_ref, f32[2048,512]{1,0:T(8,128)} %get-tuple-element.1031.adjoint_ref, f32[2048,512]{1,0:T(8,128)} %get-tuple-element.1032.conv_ref, ...), custom_call_target="tpu_custom_call" | custom-call | tf_op jit(solution)/shard_map/pallas_call | solution.py:499
  915.7 9.3 shard_map.324
  925.0 9.4 shard_map.325
  943.0 9.2 shard_map.326
  953.6 9.3 shard_map.327
  976.6 27.3 %shard_map.328 = (f32[4,192,1024]{2,1,0:T(8,128)}, f32[4,192,1024]{2,1,0:T(8,128)}) custom-call(s32[1]{0:T(128)} %bitcast.span_ref, f32[2048,1536]{1,0:T(8,128)} %multiply_multiply_fusion.refs_0_, f32[2048,512]{1,0:T(8,128)} %dynamic_update_slice.125.refs_0_.refs_1_, f32[2048,512]{1,0:T(8,128)} %get-tuple-element.1102.refs_1_.refs_2_), custom_call_target="tpu_custom_call" | custom-call | tf_op jit(solution)/shard_map/pallas_call | solution.py:564
  1006.0 15.7 %shard_map.329 = (f32[4,192,512]{2,1,0:T(8,128)}, f32[4,192,512]{2,1,0:T(8,128)}) custom-call(s32[1]{0:T(128)} %bitcast.span_ref, f32[512,1536]{1,0:T(8,128)} %copy-done.26, f32[512,1536]{1,0:T(8,128)} %copy-done.24, f32[512,1536]{1,0:T(8,128)} %copy-done.22, f32[512,1536]{1,0:T(8,128)} %copy-done.20, f32[512,512]{1,0:T(8,128)} %get-tuple-element.1110.refs_4_, ...), custom_call_target="tpu_custom_call" | custom-call | tf_op jit(solution)/shard_map/pallas_call | solution.py:564
  1042.5 32.7 %collective-permute-done.61 = f32[4,192,1024]{2,1,0:T(8,128)} collective-permute-done((f32[4,192,1024]{2,1,0:T(8,128)}, f32[4,192,1024]{2,1,0:T(8,128)}, u32[]{:S(2)}, u32[]{:S(2)}) %collective-permute-start.61) | collective-permute-done | bytes 3145760 | tf_op jit(solution)/shard_map/ppermute | solution.py:89
  1080.6 21.2 %collective-permute-done.63 = f32[256,1536]{1,0:T(8,128)} collective-permute-done((f32[256,1536]{1,0:T(8,128)}, f32[256,1536]{1,0:T(8,128)}, u32[]{:S(2)}, u32[]{:S(2)}) %collective-permute-start.63) | collective-permute-done | bytes 1572896 | tf_op jit(solution)/shard_map/ppermute | solution.py:89
  1122.7 23.3 %collective-permute-done.67 = f32[192,1024]{1,0:T(8,128)} collective-permute-done((f32[192,1024]{1,0:T(8,128)}, f32[192,1024]{1,0:T(8,128)}, u32[]{:S(2)}, u32[]{:S(2)}) %collective-permute-start.67) | collective-permute-done | bytes 786464 | tf_op jit(solution)/shard_map/ppermute | solution.py:85
  1183.6 24.1 %collective-permute-done.78 = f32[192,512]{1,0:T(8,128)S(1)} collective-permute-done((f32[192,512]{1,0:T(8,128)S(1)}, f32[192,512]{1,0:T(8,128)S(1)}, u32[]{:S(2)}, u32[]{:S(2)}) %collective-permute-start.78) | collective-permute-done | bytes 393248 | tf_op jit(solution)/shard_map/ppermute | solution.py:85
  1209.5 9.3 collective-permute-done.80
  (593 shorter events, 439.9 us)
Async XLA Ops:
  7.2 218.8 %all-gather.4.cloned.1.call-start = ((), (), s32[]{:S(2)}) async-start(), calls=%async_computation.3 | async-start | bytes 7962624 | tf_op jit(solution)/shard_map/all_gather | solution.py:184
  8.0 355.3 %all-gather.6.cloned.1.call-start = ((), (), s32[]{:S(2)}) async-start(), calls=%async_computation.4 | async-start | bytes 7962624 | tf_op jit(solution)/shard_map/all_gather | solution.py:184
  11.1 40.1 %collective-permute-start.9 = (f32[192,512]{1,0:T(8,128)}, f32[192,512]{1,0:T(8,128)}, u32[]{:S(2)}, u32[]{:S(2)}) collective-permute-start(f32[192,512]{1,0:T(8,128)} %param.20), channel_id=1, source_target_pairs={{0,4},{4,0},{1,5},{5,1},{2,6},{6,2},{3,7},{7,3},{8,12},{12,8},{9,1... | collective-permute-start | bytes 1179656 | tf_op jit(solution)/shard_map/ppermute | solution.py:89
  12.6 39.6 %collective-permute-start.3 = (f32[192,512]{1,0:T(8,128)}, f32[192,512]{1,0:T(8,128)}, u32[]{:S(2)}, u32[]{:S(2)}) collective-permute-start(f32[192,512]{1,0:T(8,128)} %param.21), channel_id=1, source_target_pairs={{0,4},{4,0},{1,5},{5,1},{2,6},{6,2},{3,7},{7,3},{8,12},{12,8},{9,1... | collective-permute-start | bytes 1179656 | tf_op jit(solution)/shard_map/ppermute | solution.py:89
  13.1 39.1 %collective-permute-start.4 = (f32[192,512]{1,0:T(8,128)}, f32[192,512]{1,0:T(8,128)}, u32[]{:S(2)}, u32[]{:S(2)}) collective-permute-start(f32[192,512]{1,0:T(8,128)} %param.22), channel_id=1, source_target_pairs={{0,4},{4,0},{1,5},{5,1},{2,6},{6,2},{3,7},{7,3},{8,12},{12,8},{9,1... | collective-permute-start | bytes 1179656 | tf_op jit(solution)/shard_map/ppermute | solution.py:89
  71.5 47.1 %collective-permute-start.5 = (f32[2,192,512]{2,1,0:T(8,128)S(1)}, f32[2,192,512]{2,1,0:T(8,128)}, u32[]{:S(2)}, u32[]{:S(2)}) collective-permute-start(f32[2,192,512]{2,1,0:T(8,128)S(1)} %pad_maximum_fusion.4), channel_id=1, source_target_pairs={{0,8},{8,16},{16,24},{24,0},{1,9},{9,17},{17,25},{25,1},{2,10},{10... | collective-permute-start | bytes 2359304 | tf_op jit(solution)/shard_map/ppermute | solution.py:85
  73.2 32.7 %collective-permute-start.7 = (f32[192,512]{1,0:T(8,128)}, f32[192,512]{1,0:T(8,128)S(1)}, u32[]{:S(2)}, u32[]{:S(2)}) collective-permute-start(f32[192,512]{1,0:T(8,128)} %collective-permute-done.1), channel_id=1, source_target_pairs={{0,4},{4,0},{1,5},{5,1},{2,6},{6,2},{3,7},{7,3},{8,12},{12,8},{9,1... | collective-permute-start | bytes 1179656 | tf_op jit(solution)/shard_map/ppermute | solution.py:89
  73.6 44.8 %collective-permute-start.8 = (f32[192,512]{1,0:T(8,128)S(1)}, f32[192,512]{1,0:T(8,128)S(1)}, u32[]{:S(2)}, u32[]{:S(2)}) collective-permute-start(f32[192,512]{1,0:T(8,128)S(1)} %collective-permute-done.2), channel_id=1, source_target_pairs={{0,4},{4,0},{1,5},{5,1},{2,6},{6,2},{3,7},{7,3},{8,12},{12,8},{9,1... | collective-permute-start | bytes 1179656 | tf_op jit(solution)/shard_map/ppermute | solution.py:89
  118.5 36.9 %collective-permute-start.10 = (f32[2,192,512]{2,1,0:T(8,128)}, f32[2,192,512]{2,1,0:T(8,128)S(1)}, u32[]{:S(2)}, u32[]{:S(2)}) collective-permute-start(f32[2,192,512]{2,1,0:T(8,128)} %collective-permute-done.5), channel_id=1, source_target_pairs={{0,8},{8,16},{16,24},{24,0},{1,9},{9,17},{17,25},{25,1},{2,10},{10... | collective-permute-start | bytes 2359304 | tf_op jit(solution)/shard_map/ppermute | solution.py:85
  163.7 35.2 %collective-permute-start.13 = (f32[3,512]{1,0:T(4,128)S(1)}, f32[3,512]{1,0:T(4,128)S(1)}, u32[]{:S(2)}, u32[]{:S(2)}) collective-permute-start(f32[3,512]{1,0:T(4,128)S(1)} %slice.265), channel_id=1, source_target_pairs={{0,4},{1,5},{2,6},{3,7},{8,12},{9,13},{10,14},{11,15},{16,20},{17,... | collective-permute-start | bytes 18440 | tf_op jit(solution)/shard_map/ppermute | solution.py:80
  255.1 217.4 %all-gather.8.cloned.1.call-start = ((), (), s32[]{:S(2)}) async-start(), calls=%async_computation.5 | async-start | bytes 7962624 | tf_op jit(solution)/shard_map/all_gather | solution.py:184
  257.5 36.4 %collective-permute-start.19 = (f32[256,1536]{1,0:T(8,128)S(1)}, f32[256,1536]{1,0:T(8,128)S(1)}, u32[]{:S(2)}, u32[]{:S(2)}) collective-permute-start(f32[256,1536]{1,0:T(8,128)S(1)} %add.674), channel_id=1, source_target_pairs={{0,2},{1,3},{2,0},{3,1},{4,6},{5,7},{6,4},{7,5},{8,10},{9,11},{10,... | collective-permute-start | bytes 4718600 | tf_op jit(solution)/shard_map/ppermute | solution.py:89
  265.6 30.4 %collective-permute-start.20 = (f32[256,1536]{1,0:T(8,128)}, f32[256,1536]{1,0:T(8,128)}, u32[]{:S(2)}, u32[]{:S(2)}) collective-permute-start(f32[256,1536]{1,0:T(8,128)} %get-tuple-element.716), channel_id=1, source_target_pairs={{0,1},{1,0},{2,3},{3,2},{4,5},{5,4},{6,7},{7,6},{8,9},{9,8},{10,11... | collective-permute-start | bytes 4718600 | tf_op jit(solution)/shard_map/ppermute | solution.py:89
  294.2 37.0 %collective-permute-start.22 = (f32[256,1536]{1,0:T(8,128)}, f32[256,1536]{1,0:T(8,128)S(1)}, u32[]{:S(2)}, u32[]{:S(2)}) collective-permute-start(f32[256,1536]{1,0:T(8,128)} %add.675), channel_id=1, source_target_pairs={{0,2},{1,3},{2,0},{3,1},{4,6},{5,7},{6,4},{7,5},{8,10},{9,11},{10,... | collective-permute-start | bytes 4718600 | tf_op jit(solution)/shard_map/ppermute | solution.py:89
  295.8 37.1 %collective-permute-start.23 = (f32[256,1536]{1,0:T(8,128)}, f32[256,1536]{1,0:T(8,128)S(1)}, u32[]{:S(2)}, u32[]{:S(2)}) collective-permute-start(f32[256,1536]{1,0:T(8,128)} %get-tuple-element.723), channel_id=1, source_target_pairs={{0,1},{1,0},{2,3},{3,2},{4,5},{5,4},{6,7},{7,6},{8,9},{9,8},{10,11... | collective-permute-start | bytes 4718600 | tf_op jit(solution)/shard_map/ppermute | solution.py:89
  363.3 368.2 %reduce-scatter.4.cloned.1.call-start = ((), (), s32[]{:S(2)}) async-start(), calls=%async_computation.6 | async-start | bytes 7962624 | tf_op jit(solution)/shard_map/reduce_scatter | solution.py:723
  363.4 36.0 %collective-permute-start.25 = (f32[256,1536]{1,0:T(8,128)}, f32[256,1536]{1,0:T(8,128)S(1)}, u32[]{:S(2)}, u32[]{:S(2)}) collective-permute-start(f32[256,1536]{1,0:T(8,128)} %add.679), channel_id=1, source_target_pairs={{0,2},{1,3},{2,0},{3,1},{4,6},{5,7},{6,4},{7,5},{8,10},{9,11},{10,... | collective-permute-start | bytes 4718600 | tf_op jit(solution)/shard_map/ppermute | solution.py:89
  399.7 41.8 %collective-permute-start.27 = (f32[256,1536]{1,0:T(8,128)}, f32[256,1536]{1,0:T(8,128)}, u32[]{:S(2)}, u32[]{:S(2)}) collective-permute-start(f32[256,1536]{1,0:T(8,128)} %add.683), channel_id=1, source_target_pairs={{0,2},{1,3},{2,0},{3,1},{4,6},{5,7},{6,4},{7,5},{8,10},{9,11},{10,... | collective-permute-start | bytes 4718600 | tf_op jit(solution)/shard_map/ppermute | solution.py:89
  531.8 358.6 %reduce-scatter.6.cloned.1.call-start = ((), (), s32[]{:S(2)}) async-start(), calls=%async_computation.7 | async-start | bytes 7962624 | tf_op jit(solution)/shard_map/reduce_scatter | solution.py:723
  531.9 37.0 %collective-permute-start.31 = (f32[256,1536]{1,0:T(8,128)}, f32[256,1536]{1,0:T(8,128)S(1)}, u32[]{:S(2)}, u32[]{:S(2)}) collective-permute-start(f32[256,1536]{1,0:T(8,128)} %add.708), channel_id=1, source_target_pairs={{0,2},{1,3},{2,0},{3,1},{4,6},{5,7},{6,4},{7,5},{8,10},{9,11},{10,... | collective-permute-start | bytes 4718600 | tf_op jit(solution)/shard_map/ppermute | solution.py:89
  570.3 41.7 %collective-permute-start.34 = (f32[256,1536]{1,0:T(8,128)}, f32[256,1536]{1,0:T(8,128)}, u32[]{:S(2)}, u32[]{:S(2)}) collective-permute-start(f32[256,1536]{1,0:T(8,128)} %add.709), channel_id=1, source_target_pairs={{0,2},{1,3},{2,0},{3,1},{4,6},{5,7},{6,4},{7,5},{8,10},{9,11},{10,... | collective-permute-start | bytes 4718600 | tf_op jit(solution)/shard_map/ppermute | solution.py:89
  614.8 36.7 %collective-permute-start.37 = (f32[256,1536]{1,0:T(8,128)}, f32[256,1536]{1,0:T(8,128)}, u32[]{:S(2)}, u32[]{:S(2)}) collective-permute-start(f32[256,1536]{1,0:T(8,128)} %add.711), channel_id=1, source_target_pairs={{0,2},{1,3},{2,0},{3,1},{4,6},{5,7},{6,4},{7,5},{8,10},{9,11},{10,... | collective-permute-start | bytes 4718600 | tf_op jit(solution)/shard_map/ppermute | solution.py:89
  653.7 41.5 %collective-permute-start.40 = (f32[256,1536]{1,0:T(8,128)}, f32[256,1536]{1,0:T(8,128)}, u32[]{:S(2)}, u32[]{:S(2)}) collective-permute-start(f32[256,1536]{1,0:T(8,128)} %add.714), channel_id=1, source_target_pairs={{0,2},{1,3},{2,0},{3,1},{4,6},{5,7},{6,4},{7,5},{8,10},{9,11},{10,... | collective-permute-start | bytes 4718600 | tf_op jit(solution)/shard_map/ppermute | solution.py:89
  731.5 304.4 %reduce-scatter.8.cloned.1.call-start = ((), (), s32[]{:S(2)}) async-start(), calls=%async_computation.8 | async-start | bytes 7962624 | tf_op jit(solution)/shard_map/reduce_scatter | solution.py:723
  732.2 36.7 %collective-permute-start.43 = (f32[256,1536]{1,0:T(8,128)}, f32[256,1536]{1,0:T(8,128)S(1)}, u32[]{:S(2)}, u32[]{:S(2)}) collective-permute-start(f32[256,1536]{1,0:T(8,128)} %add.717), channel_id=1, source_target_pairs={{0,2},{1,3},{2,0},{3,1},{4,6},{5,7},{6,4},{7,5},{8,10},{9,11},{10,... | collective-permute-start | bytes 4718600 | tf_op jit(solution)/shard_map/ppermute | solution.py:89
  769.1 74.1 %collective-permute-start.47 = (f32[256,1536]{1,0:T(8,128)}, f32[256,1536]{1,0:T(8,128)}, u32[]{:S(2)}, u32[]{:S(2)}) collective-permute-start(f32[256,1536]{1,0:T(8,128)} %add.720), channel_id=1, source_target_pairs={{0,2},{1,3},{2,0},{3,1},{4,6},{5,7},{6,4},{7,5},{8,10},{9,11},{10,... | collective-permute-start | bytes 4718600 | tf_op jit(solution)/shard_map/ppermute | solution.py:89
  780.3 65.3 %collective-permute-start.48 = (f32[256,1536]{1,0:T(8,128)}, f32[256,1536]{1,0:T(8,128)}, u32[]{:S(2)}, u32[]{:S(2)}) collective-permute-start(f32[256,1536]{1,0:T(8,128)} %get-tuple-element.960), channel_id=1, source_target_pairs={{0,1},{1,0},{2,3},{3,2},{4,5},{5,4},{6,7},{7,6},{8,9},{9,8},{10,11... | collective-permute-start | bytes 4718600 | tf_op jit(solution)/shard_map/ppermute | solution.py:89
  783.4 56.6 %collective-permute-start.46 = (f32[256,1536]{1,0:T(8,128)}, f32[256,1536]{1,0:T(8,128)}, u32[]{:S(2)}, u32[]{:S(2)}) collective-permute-start(f32[256,1536]{1,0:T(8,128)} %add.723), channel_id=1, source_target_pairs={{0,2},{1,3},{2,0},{3,1},{4,6},{5,7},{6,4},{7,5},{8,10},{9,11},{10,... | collective-permute-start | bytes 4718600 | tf_op jit(solution)/shard_map/ppermute | solution.py:89
  847.3 36.8 %collective-permute-start.50 = (f32[256,1536]{1,0:T(8,128)S(1)}, f32[256,1536]{1,0:T(8,128)S(1)}, u32[]{:S(2)}, u32[]{:S(2)}) collective-permute-start(f32[256,1536]{1,0:T(8,128)S(1)} %add.727), channel_id=1, source_target_pairs={{0,2},{1,3},{2,0},{3,1},{4,6},{5,7},{6,4},{7,5},{8,10},{9,11},{10,... | collective-permute-start | bytes 4718600 | tf_op jit(solution)/shard_map/ppermute | solution.py:89
  963.5 58.1 %collective-permute-start.57 = (f32[256,1536]{1,0:T(8,128)S(1)}, f32[256,1536]{1,0:T(8,128)}, u32[]{:S(2)}, u32[]{:S(2)}) collective-permute-start(f32[256,1536]{1,0:T(8,128)S(1)} %copy-done.43), channel_id=1, source_target_pairs={{0,1},{1,0},{2,3},{3,2},{4,5},{5,4},{6,7},{7,6},{8,9},{9,8},{10,11... | collective-permute-start | bytes 4718600 | tf_op jit(solution)/shard_map/ppermute | solution.py:89
  963.6 62.8 %collective-permute-start.58 = (f32[256,1536]{1,0:T(8,128)S(1)}, f32[256,1536]{1,0:T(8,128)}, u32[]{:S(2)}, u32[]{:S(2)}) collective-permute-start(f32[256,1536]{1,0:T(8,128)S(1)} %add.729), channel_id=1, source_target_pairs={{0,1},{1,0},{2,3},{3,2},{4,5},{5,4},{6,7},{7,6},{8,9},{9,8},{10,11... | collective-permute-start | bytes 4718600 | tf_op jit(solution)/shard_map/ppermute | solution.py:89
  964.0 68.1 %collective-permute-start.59 = (f32[256,1536]{1,0:T(8,128)}, f32[256,1536]{1,0:T(8,128)}, u32[]{:S(2)}, u32[]{:S(2)}) collective-permute-start(f32[256,1536]{1,0:T(8,128)} %add.730), channel_id=1, source_target_pairs={{0,2},{1,3},{2,0},{3,1},{4,6},{5,7},{6,4},{7,5},{8,10},{9,11},{10,... | collective-permute-start | bytes 4718600 | tf_op jit(solution)/shard_map/ppermute | solution.py:89
  964.2 75.0 %collective-permute-start.60 = (f32[256,1536]{1,0:T(8,128)}, f32[256,1536]{1,0:T(8,128)}, u32[]{:S(2)}, u32[]{:S(2)}) collective-permute-start(f32[256,1536]{1,0:T(8,128)} %add.734), channel_id=1, source_target_pairs={{0,2},{1,3},{2,0},{3,1},{4,6},{5,7},{6,4},{7,5},{8,10},{9,11},{10,... | collective-permute-start | bytes 4718600 | tf_op jit(solution)/shard_map/ppermute | solution.py:89
  1003.9 71.3 %collective-permute-start.61 = (f32[4,192,1024]{2,1,0:T(8,128)}, f32[4,192,1024]{2,1,0:T(8,128)}, u32[]{:S(2)}, u32[]{:S(2)}) collective-permute-start(f32[4,192,1024]{2,1,0:T(8,128)} %get-tuple-element.1134), channel_id=1, source_target_pairs={{0,4},{4,0},{1,5},{5,1},{2,6},{6,2},{3,7},{7,3},{8,12},{12,8},{9,1... | collective-permute-start | bytes 9437192 | tf_op jit(solution)/shard_map/ppermute | solution.py:89
  1021.7 59.0 %collective-permute-start.62 = (f32[256,1536]{1,0:T(8,128)}, f32[256,1536]{1,0:T(8,128)}, u32[]{:S(2)}, u32[]{:S(2)}) collective-permute-start(f32[256,1536]{1,0:T(8,128)} %add.735), channel_id=1, source_target_pairs={{0,2},{1,3},{2,0},{3,1},{4,6},{5,7},{6,4},{7,5},{8,10},{9,11},{10,... | collective-permute-start | bytes 4718600 | tf_op jit(solution)/shard_map/ppermute | solution.py:89
  1026.4 75.5 %collective-permute-start.63 = (f32[256,1536]{1,0:T(8,128)}, f32[256,1536]{1,0:T(8,128)}, u32[]{:S(2)}, u32[]{:S(2)}) collective-permute-start(f32[256,1536]{1,0:T(8,128)} %add.743), channel_id=1, source_target_pairs={{0,2},{1,3},{2,0},{3,1},{4,6},{5,7},{6,4},{7,5},{8,10},{9,11},{10,... | collective-permute-start | bytes 4718600 | tf_op jit(solution)/shard_map/ppermute | solution.py:89
  1032.2 75.3 %collective-permute-start.64 = (f32[4,192,512]{2,1,0:T(8,128)}, f32[4,192,512]{2,1,0:T(8,128)}, u32[]{:S(2)}, u32[]{:S(2)}) collective-permute-start(f32[4,192,512]{2,1,0:T(8,128)} %get-tuple-element.1115), channel_id=1, source_target_pairs={{0,4},{4,0},{1,5},{5,1},{2,6},{6,2},{3,7},{7,3},{8,12},{12,8},{9,1... | collective-permute-start | bytes 4718600 | tf_op jit(solution)/shard_map/ppermute | solution.py:89
  1039.2 109.7 %collective-permute-start.69 = (f32[256,1536]{1,0:T(8,128)}, f32[256,1536]{1,0:T(8,128)}, u32[]{:S(2)}, u32[]{:S(2)}) collective-permute-start(f32[256,1536]{1,0:T(8,128)} %add.748), channel_id=1, source_target_pairs={{0,1},{1,0},{2,3},{3,2},{4,5},{5,4},{6,7},{7,6},{8,9},{9,8},{10,11... | collective-permute-start | bytes 4718600 | tf_op jit(solution)/shard_map/ppermute | solution.py:89
  1079.0 42.8 %collective-permute-start.68 = (f32[192,1024]{1,0:T(8,128)}, f32[192,1024]{1,0:T(8,128)S(1)}, u32[]{:S(2)}, u32[]{:S(2)}) collective-permute-start(f32[192,1024]{1,0:T(8,128)} %get-tuple-element.1151), channel_id=1, source_target_pairs={{0,24},{8,0},{16,8},{24,16},{1,25},{9,1},{17,9},{25,17},{2,26},{10... | collective-permute-start | bytes 2359304 | tf_op jit(solution)/shard_map/ppermute | solution.py:85
  1080.6 65.3 %collective-permute-start.67 = (f32[192,1024]{1,0:T(8,128)}, f32[192,1024]{1,0:T(8,128)}, u32[]{:S(2)}, u32[]{:S(2)}) collective-permute-start(f32[192,1024]{1,0:T(8,128)} %get-tuple-element.1173), channel_id=1, source_target_pairs={{0,16},{8,24},{16,0},{24,8},{1,17},{9,25},{17,1},{25,9},{2,18},{10... | collective-permute-start | bytes 2359304 | tf_op jit(solution)/shard_map/ppermute | solution.py:85
  1101.9 44.1 %collective-permute-start.66 = (f32[192,1024]{1,0:T(8,128)}, f32[192,1024]{1,0:T(8,128)}, u32[]{:S(2)}, u32[]{:S(2)}) collective-permute-start(f32[192,1024]{1,0:T(8,128)} %get-tuple-element.1172), channel_id=1, source_target_pairs={{0,8},{8,16},{16,24},{24,0},{1,9},{9,17},{17,25},{25,1},{2,10},{10... | collective-permute-start | bytes 2359304 | tf_op jit(solution)/shard_map/ppermute | solution.py:85
  1120.7 38.3 %collective-permute-start.71 = (f32[256,1536]{1,0:T(8,128)S(1)}, f32[256,1536]{1,0:T(8,128)}, u32[]{:S(2)}, u32[]{:S(2)}) collective-permute-start(f32[256,1536]{1,0:T(8,128)S(1)} %copy-done.44), channel_id=1, source_target_pairs={{0,1},{1,0},{2,3},{3,2},{4,5},{5,4},{6,7},{7,6},{8,9},{9,8},{10,11... | collective-permute-start | bytes 4718600 | tf_op jit(solution)/shard_map/ppermute | solution.py:89
  1121.8 46.9 %collective-permute-start.74 = (f32[256,1536]{1,0:T(8,128)S(1)}, f32[256,1536]{1,0:T(8,128)}, u32[]{:S(2)}, u32[]{:S(2)}) collective-permute-start(f32[256,1536]{1,0:T(8,128)S(1)} %add.767), channel_id=1, source_target_pairs={{0,1},{1,0},{2,3},{3,2},{4,5},{5,4},{6,7},{7,6},{8,9},{9,8},{10,11... | collective-permute-start | bytes 4718600 | tf_op jit(solution)/shard_map/ppermute | solution.py:89
  1146.0 31.7 %collective-permute-start.76 = (f32[256,1536]{1,0:T(8,128)S(1)}, f32[256,1536]{1,0:T(8,128)S(1)}, u32[]{:S(2)}, u32[]{:S(2)}) collective-permute-start(f32[256,1536]{1,0:T(8,128)S(1)} %add.768), channel_id=1, source_target_pairs={{0,1},{1,0},{2,3},{3,2},{4,5},{5,4},{6,7},{7,6},{8,9},{9,8},{10,11... | collective-permute-start | bytes 4718600 | tf_op jit(solution)/shard_map/ppermute | solution.py:89
  1166.6 41.0 %collective-permute-start.78 = (f32[192,512]{1,0:T(8,128)S(1)}, f32[192,512]{1,0:T(8,128)S(1)}, u32[]{:S(2)}, u32[]{:S(2)}) collective-permute-start(f32[192,512]{1,0:T(8,128)S(1)} %copy-done.72), channel_id=1, source_target_pairs={{0,16},{8,24},{16,0},{24,8},{1,17},{9,25},{17,1},{25,9},{2,18},{10... | collective-permute-start | bytes 1179656 | tf_op jit(solution)/shard_map/ppermute | solution.py:85
  1167.8 39.9 %collective-permute-start.77 = (f32[192,512]{1,0:T(8,128)S(1)}, f32[192,512]{1,0:T(8,128)S(1)}, u32[]{:S(2)}, u32[]{:S(2)}) collective-permute-start(f32[192,512]{1,0:T(8,128)S(1)} %get-tuple-element.1228), channel_id=1, source_target_pairs={{0,8},{8,16},{16,24},{24,0},{1,9},{9,17},{17,25},{25,1},{2,10},{10... | collective-permute-start | bytes 1179656 | tf_op jit(solution)/shard_map/ppermute | solution.py:85
  1175.3 43.6 %collective-permute-start.80 = (f32[1068,128]{1,0:T(8,128)S(1)}, f32[1068,128]{1,0:T(8,128)S(1)}, u32[]{:S(2)}, u32[]{:S(2)}) collective-permute-start(f32[1068,128]{1,0:T(8,128)S(1)} %add.784), channel_id=1, source_target_pairs={{0,16},{8,24},{16,0},{24,8},{1,17},{9,25},{17,1},{25,9},{2,18},{10... | collective-permute-start | bytes 1640456 | tf_op jit(solution)/shard_map/ppermute | solution.py:89
  1177.7 41.3 %collective-permute-start.81 = (f32[12,128]{1,0:T(8,128)S(1)}, f32[12,128]{1,0:T(8,128)S(1)}, u32[]{:S(2)}, u32[]{:S(2)}) collective-permute-start(f32[12,128]{1,0:T(8,128)S(1)} %add.787), channel_id=1, source_target_pairs={{0,8},{8,0},{16,24},{24,16},{1,9},{9,1},{17,25},{25,17},{2,10},{10... | collective-permute-start | bytes 18440 | tf_op jit(solution)/shard_map/ppermute | solution.py:89
  (152 other events, 2137.9 us)
Sparse Core Ops, SparseCore 0:
  10.2 160.6 all-gather.3
  255.3 107.9 all-gather.5
  365.5 106.9 all-gather.7
  532.0 127.2 reduce-scatter.3
  731.7 126.7 reduce-scatter.5
  890.6 126.4 reduce-scatter.7
